TPU v7x, 128 devices: a whole 4x4x4 slice. The times are simulated.
128 devices in a mesh: row: 8 (over y_lo, x), col: 16 (over y_hi, z, core).
Axes of the slice: x: 4, y: 4 (y_hi: 2, y_lo: 2; y = y_hi * 2 + y_lo), z: 4, core: 2. Of those that a mesh axis runs over, the one named last changes fastest.
Arguments:
- known_inverse: float32 [7168, 7168], P('col', 'row'), may hold values from -6 to 6
- factor_panel: float32 [7168, 4096], P('col', 'row'), may hold values from -0.0625 to 0.0625
- diag_base: float32 [4096, 4096], P('row', 'col'), may hold values from -6 to 6
- ancestor_map: int32 [28], replicated, may hold values from 0 to 27, each once
Outputs:
- new_column: float32 [7168, 4096], P('col', 'row')
- diagonal_block: float32 [4096, 4096], P('row', 'col')
Inputs may be any that keep to these rules, and one draw needn't show every extreme that they name: `ancestor_map`: a permutation of the 28 ancestor blocks.
All inputs are finite; a program needn't handle non-finite values.
Results may differ from a plain program's by a relative error of at most 0.000071.
Values sent between devices are 32-bit elements; how exact they have to be, the bound alone decides.
A program may use at most 128 MiB of HBM per device.

v0:
```python
import jax
import jax.numpy as jnp
from jax import lax
from jax.sharding import PartitionSpec as P


def on_device(known_inverse, factor_panel, diag_base, ancestor_map):
    panel = lax.all_gather(factor_panel, "col", axis=0, tiled=True)
    block_count = ancestor_map.shape[0]
    block_rows = panel.shape[0] // block_count
    inverse = (
        jnp.zeros((block_count,), jnp.int32)
        .at[ancestor_map]
        .set(jnp.arange(block_count, dtype=jnp.int32))
    )
    placed = jnp.take(
        panel.reshape(block_count, block_rows, panel.shape[1]), inverse, axis=0
    ).reshape(panel.shape)
    product = jnp.dot(
        lax.all_gather(known_inverse, "row", axis=1, tiled=True),
        placed,
        precision=lax.Precision.HIGHEST,
        preferred_element_type=jnp.float32,
    )
    new_column = -product
    own_count = known_inverse.shape[0]
    own_start = lax.axis_index("col") * own_count
    own_rows = lax.dynamic_slice_in_dim(placed, own_start, own_count, 0)
    spread_rows = lax.all_gather(new_column, "row", axis=1, tiled=True)
    reduced = lax.psum_scatter(
        lax.dot_general(
            spread_rows,
            own_rows,
            (((0,), (0,)), ((), ())),
            precision=lax.Precision.HIGHEST,
            preferred_element_type=jnp.float32,
        ),
        "col",
        scatter_dimension=0,
        tiled=True,
    )
    diagonal_block = diag_base - reduced.T
    return (new_column, diagonal_block)


def solution(mesh):
    placed = (P("col", "row"), P("col", "row"), P("row", "col"), P())
    return jax.shard_map(
        on_device,
        mesh=mesh,
        in_specs=placed,
        out_specs=(P("col", "row"), P("row", "col")),
        check_vma=False,
    )
```

profile of v0, /device:TPU:1, one launch (start us, length us, event | category | flops | bytes accessed | tf_op | source)
XLA Modules:
  0.0 479.7 jit_solution(4137999078378391035)
XLA Ops:
  7.2 0.0 all-gather.4.cloned.1.call-start
  7.2 0.7 all-gather.4.cloned.1.call-update
  7.9 0.0 all-gather.6.cloned.1.call-start
  7.9 0.7 all-gather.6.cloned.1.call-update
  8.6 0.0 all-gather.8.cloned.1.call-start
  8.7 0.7 compare_select_fusion.1
  9.4 0.7 scatter_custom_fusion
  10.0 0.1 broadcast_in_dim.20
  10.2 103.8 %all-gather.4.cloned.1.call-done = f32[7168,512]{1,0:T(8,128)} async-done(((f32[448,512]{1,0:T(8,128)}), f32[7168,512]{1,0:T(8,128)}) %all-gather.4.cloned.1.call-update) | async-done | bytes 14680080 | tf_op jit(solution)/shard_map/all_gather | solution.py:8
  114.0 13.1 %gather_fusion = f32[28,256,512]{2,1,0:T(8,128)} fusion(f32[28,256,512]{2,1,0:T(8,128)} %bitcast.10, s32[1024]{0:T(1024)S(1)} %pad_clamp_fusion), kind=kCustom, calls=%fused_computation | custom fusion | bytes 29360240 | tf_op jit(solution)/shard_map/jit(_take)/gather | solution.py:16
  127.1 11.6 %bitcast_select_fusion = f32[7168,512]{1,0:T(8,128)} fusion(f32[28,256,512]{2,1,0:T(8,128)} %gather_fusion, pred[7168]{0:T(1024)(128)(4,1)S(1)} %broadcast_in_dim.21), kind=kLoop, calls=%fused_computation.2 | loop fusion | flops 3670016 | bytes 29367296 | tf_op jit(solution)/shard_map/jit(_take)/select_n | solution.py:16
  138.6 107.8 %all-gather.6.cloned.1.call-done = f32[448,7168]{1,0:T(8,128)} async-done(((f32[448,896]{1,0:T(8,128)}), f32[448,7168]{1,0:T(8,128)}) %all-gather.6.cloned.1.call-update) | async-done | bytes 12845072 | tf_op jit(solution)/shard_map/all_gather | solution.py:20
  246.4 25.3 %fusion = f32[448,512]{1,0:T(8,128)} fusion(f32[7168,512]{1,0:T(8,128)} %bitcast_select_fusion, f32[448,7168]{1,0:T(8,128)} %all-gather.6.cloned.1.call-done), kind=kOutput, calls=%fused_computation.4 | convolution fusion | flops 19730235392 | bytes 28442624 | tf_op jit(solution)/shard_map/dot_general | solution.py:19
  271.7 0.0 all-gather.8.cloned.1.call-update
  271.7 0.2 reduce-scatter.2.cloned.1.call-start
  272.0 0.0 copy-start
  272.0 80.8 %all-gather.8.cloned.1.call-done = f32[448,4096]{1,0:T(8,128)} async-done(((f32[448,512]{1,0:T(8,128)}), f32[448,4096]{1,0:T(8,128)}) %all-gather.8.cloned.1.call-update) | async-done | bytes 7340048 | tf_op jit(solution)/shard_map/all_gather | solution.py:29
  352.7 18.0 %fusion.1 = f32[4096,512]{1,0:T(8,128)} fusion(f32[448,4096]{1,0:T(8,128)} %all-gather.8.cloned.1.call-done, f32[7168,512]{1,0:T(8,128)} %bitcast_select_fusion, s32[]{:T(128)S(6)} %select_n.19), kind=kOutput, calls=%fused_computation.5 | convolution fusion | flops 11274289152 | bytes 16646148 | tf_op jit(solution)/shard_map/dot_general | solution.py:31
  370.7 0.0 reduce-scatter.2.cloned.1.call-update
  370.7 0.0 copy-done
  370.7 0.2 copy.6
  370.9 100.1 %reduce-scatter.2.cloned.1.call-done = f32[256,512]{1,0:T(8,128)} async-done(((f32[4096,512]{1,0:T(8,128)}), f32[256,512]{1,0:T(8,128)}) %reduce-scatter.2.cloned.1.call-update) | async-done | bytes 524304 | tf_op jit(solution)/shard_map/reduce_scatter | solution.py:30
  471.1 1.1 bitcast_subtract_fusion
  472.2 1.0 copy.7
  (5 shorter events, 0.0 us)
Async XLA Ops:
  7.2 106.8 %all-gather.4.cloned.1.call-start = ((), (), s32[]{:S(2)}) async-start(), calls=%async_computation.1 | async-start | bytes 15597568 | tf_op jit(solution)/shard_map/all_gather | solution.py:8
  7.9 238.5 %all-gather.6.cloned.1.call-start = ((), (), s32[]{:S(2)}) async-start(), calls=%async_computation.2 | async-start | bytes 14450688 | tf_op jit(solution)/shard_map/all_gather | solution.py:20
  8.6 344.1 %all-gather.8.cloned.1.call-start = ((), (), s32[]{:S(2)}) async-start(), calls=%async_computation.3 | async-start | bytes 8257536 | tf_op jit(solution)/shard_map/all_gather | solution.py:29
  271.7 199.4 %reduce-scatter.2.cloned.1.call-start = ((), (), s32[]{:S(2)}) async-start(), calls=%async_computation.4 | async-start | bytes 8912896 | tf_op jit(solution)/shard_map/reduce_scatter | solution.py:30
  272.0 98.8 %copy-start = (f32[512,256]{1,0:T(8,128)S(1)}, f32[512,256]{1,0:T(8,128)}, u32[]{:S(2)}) copy-start(f32[512,256]{1,0:T(8,128)} %param.6) | copy-start | bytes 1572868
Sparse Core Ops, SparseCore 0:
  10.5 103.4 all-gather.3
  115.6 130.7 all-gather.5
  271.8 80.8 all-gather.7
  370.8 100.1 reduce-scatter.1
where the time goes:
time: 480 us
  waiting for transfers between devices  394 us (82%)
  matrix products  43.2 us (9%)
  local copies, waits for them, and re-layouts  15 us (3%)
  between operations  13.8 us (3%)
  other arithmetic  13.4 us (3%)
    all_gather x1, waiting for transfers between devices, on_device(): lax.all_gather(known_inverse, 'row', axis=1, tiled=True)  108 us
    all_gather x1, waiting for transfers between devices, on_device(): panel = lax.all_gather(factor_panel, 'col', axis=0, tiled=True)  104 us
    reduce_scatter x1, waiting for transfers between devices, on_device(): lax.psum_scatter(lax.dot_general(spread_rows, own_rows, (((0,), (0,)), ((...  100 us
    all_gather x1, waiting for transfers between devices, on_device(): spread_rows = lax.all_gather(new_column, 'row', axis=1, tiled=True)  80.8 us
    dot_general x1, matrix products, on_device(): jnp.dot(lax.all_gather(known_inverse, 'row', axis=1, tiled=True), placed,...  25.3 us
    dot_general x1, matrix products, on_device(): lax.dot_general(spread_rows, own_rows, (((0,), (0,)), ((), ())), precisio...  18 us
    gather x1, local copies, waits for them, and re-layouts, on_device(): jnp.take(panel.reshape(block_count, block_rows, panel.shape[1]), inverse,...  13.1 us
    select_n x2, other arithmetic, on_device(): jnp.take(panel.reshape(block_count, block_rows, panel.shape[1]), inverse,...  11.6 us
  transfers between devices with their start and end apart: 4, of which 4 were waited for; matrix products, arithmetic and copies ran while one was open for 5% of the time, Pallas kernels for 0%

commit v1 on v0

v1 whole, which is shorter than its diff:
```python
import functools

import jax
import jax.numpy as jnp
from jax import lax
from jax.experimental import pallas as pl
from jax.experimental.pallas import tpu as pltpu
from jax.sharding import PartitionSpec as P

MESH = pl.DeviceIdType.MESH
BF = jnp.bfloat16
F32 = jnp.float32

OWN_Y, OWN_UP, OWN_DOWN, FAR_UP, FAR_DOWN, OWN_HALF_UP, OWN_HALF_DOWN, FAR_HALF_UP, FAR_HALF_DOWN, CORE = range(10)


def split(value):
    high = value.astype(BF)
    return high, (value - high.astype(F32)).astype(BF)


def three(a_high, a_low, b_high, b_low):
    def dot(a, b):
        return jnp.dot(a, b, preferred_element_type=F32)

    return dot(a_high, b_high) + (dot(a_high, b_low) + dot(a_low, b_high))


def kernel(
    inv_ref, k_ref, f_ref, n_ref, d_ref,
    k_other, k_high, k_low, sent, picked, panel, p_high, p_low,
    n_part, n_got, n_rows, t_high, t_low, d_part, d_got,
    k_sem, one_send, one_recv, two_send, two_recv, gather_send, gather_recv,
    n_send, n_recv, turn_send, turn_recv, side_send, side_recv, d_send, d_recv, local_sem,
):
    row, col = lax.axis_index("row"), lax.axis_index("col")
    x, y_lo = row % 4, row // 4
    core, z, y_hi = col % 2, (col // 2) % 4, col // 8
    own = y_hi * 4 + z
    up, down = (z + 1) % 4, (z + 3) % 4

    def at(y_hi_, z_, core_, y_lo_, x_):
        return (y_lo_ * 4 + x_, y_hi_ * 8 + z_ * 2 + core_)

    def remote(src, dst, send, recv, device):
        return pltpu.make_async_remote_copy(
            src_ref=src, dst_ref=dst, send_sem=send, recv_sem=recv, device_id=device, device_id_type=MESH
        )

    stays = jnp.logical_and(y_hi == y_lo, z == x)
    row_partner = (1 - y_lo) * 4 + x

    barrier = pltpu.get_barrier_semaphore()

    def greet(device):
        pl.semaphore_signal(barrier, inc=1, device_id=device, device_id_type=MESH)

    @pl.loop(1, 16)
    def _(k):
        greet((row, (col + k) % 16))

    @pl.loop(1, 4)
    def _(k):
        greet((y_lo * 4 + (x + k) % 4, col))

    greet((row_partner, col))
    for g in range(2):
        away = jnp.logical_not(jnp.logical_and(stays, core == g))

        @pl.when(away)
        def _():
            greet(at(y_lo, x, g, y_hi, z))

    pl.semaphore_wait(barrier, 21 - stays.astype(jnp.int32))

    k_copy = remote(k_ref, k_other, k_sem.at[0], k_sem.at[1], (row_partner, col))

    def first(k):
        to = (col + k) % 16
        src = f_ref.at[:, to // 2, :, pl.ds(pl.multiple_of((to % 2) * 256, 256), 256)]
        return remote(src, sent.at[pl.ds(col * 7, 7)], one_send.at[k], one_recv.at[k], (row, to))

    @pl.loop(1, 16)
    def _(k):
        first(k).start()

    k_copy.start()
    mine = pltpu.make_async_copy(
        f_ref.at[:, own, :, pl.ds(pl.multiple_of(core * 256, 256), 256)], sent.at[pl.ds(col * 7, 7)], local_sem.at[0]
    )
    mine.start()

    @pl.when(y_lo == 0)
    def _():
        k_high[:, 0:896], k_low[:, 0:896] = split(k_ref[...])

    @pl.when(y_lo == 1)
    def _():
        k_high[:, 896:1792], k_low[:, 896:1792] = split(k_ref[...])

    mine.wait()

    @pl.loop(1, 16)
    def _(k):
        first(k).wait_recv()

    for k in range(56):
        start = inv_ref[k // 2] * 4 + (k % 2) * 2
        to, pos = (k % 28) // 7, (k // 28) * 14 + (k % 7) * 2
        picked[to, pos : pos + 2] = sent[pl.ds(start, 2)]

    def piece(block, member, chunk=0, chunks=28):
        return panel.at[block, core, pl.ds(chunk, chunks), pl.ds(pl.multiple_of(member * 8, 8), 8), :]

    def second(k):
        to = (x + 4 - k) % 4
        return remote(picked.at[to], piece(x, own), two_send.at[k], two_recv.at[k], (y_lo * 4 + to, col))

    @pl.loop(1, 4)
    def _(k):
        second(k).start()

    keep = pltpu.make_async_copy(picked.at[x], piece(x, own), local_sem.at[1])
    keep.start()

    far = (1 - y_hi) * 4

    def gather(kind, i):
        block = (x + i + 1) % 4
        near = y_hi * 4
        high_z = at(y_hi, up, core, y_lo, x)
        low_z = at(y_hi, down, core, y_lo, x)
        if kind == CORE:
            ref, to = panel.at[block, core], (row, y_hi * 8 + z * 2 + 1 - core)
        else:
            ref, to = {
                OWN_Y: (piece(block, own), at(1 - y_hi, z, core, y_lo, x)),
                OWN_UP: (piece(block, own), high_z),
                OWN_DOWN: (piece(block, own), low_z),
                FAR_UP: (piece(block, far + z), high_z),
                FAR_DOWN: (piece(block, far + z), low_z),
                OWN_HALF_UP: (piece(block, near + down, 0, 14), high_z),
                OWN_HALF_DOWN: (piece(block, near + up, 14, 14), low_z),
                FAR_HALF_UP: (piece(block, far + down, 0, 14), high_z),
                FAR_HALF_DOWN: (piece(block, far + up, 14, 14), low_z),
            }[kind]
        return remote(ref, ref, gather_send.at[kind, i], gather_recv.at[kind, i], to)

    def own_sends(i):
        for kind in (OWN_Y, OWN_UP, OWN_DOWN):
            gather(kind, i).start()

    @pl.loop(0, 3)
    def _(i):
        second(i + 1).wait_recv()
        own_sends(i)

    keep.wait()
    own_sends(3)

    k_copy.wait_recv()

    @pl.when(y_lo == 0)
    def _():
        k_high[:, 896:1792], k_low[:, 896:1792] = split(k_other[...])

    @pl.when(y_lo == 1)
    def _():
        k_high[:, 0:896], k_low[:, 0:896] = split(k_other[...])

    def n_copy(i, turn):
        to = (x + i + 1) % 4
        return remote(
            n_part.at[i, turn], n_got.at[i, turn], n_send.at[i, turn], n_recv.at[i, turn], (y_lo * 4 + to, col)
        )

    def n_unit(i, turn):
        block = (x + i + 1) % 4
        half = (core + turn) % 2

        @pl.loop(0, 7)
        def _(k):
            value = panel[block, half, pl.ds(k * 4, 4)].reshape(256, 256)
            rows = pl.ds(pl.multiple_of(k * 256, 256), 256)
            p_high[block, half, rows], p_low[block, half, rows] = split(value)

        n_part[i, turn] = three(k_high[...], k_low[...], p_high[block, half], p_low[block, half])

        @pl.when(i < 3)
        def _():
            n_copy(i, turn).start()

    @pl.loop(0, 6)
    def _(t):
        @pl.when(t < 4)
        def _():
            gather(OWN_Y, t).wait_recv()
            gather(FAR_UP, t).start()
            gather(FAR_DOWN, t).start()

        @pl.when(jnp.logical_and(t >= 1, t < 5))
        def _():
            for arrived, passed in (
                (OWN_UP, OWN_HALF_UP), (OWN_DOWN, OWN_HALF_DOWN),
                (FAR_UP, FAR_HALF_UP), (FAR_DOWN, FAR_HALF_DOWN),
            ):
                gather(arrived, t - 1).wait_recv()
                gather(passed, t - 1).start()

        @pl.when(t >= 2)
        def _():
            i = t - 2
            for kind in (OWN_HALF_UP, OWN_HALF_DOWN, FAR_HALF_UP, FAR_HALF_DOWN):
                gather(kind, i).wait_recv()
            gather(CORE, i).start()
            n_unit(i, 0)
            gather(CORE, i).wait_recv()
            n_unit(i, 1)

    def turned(g):
        slot = pl.ds(pl.multiple_of((y_hi * 2 + core) * 448, 64), 448)
        return n_ref.at[:, pl.ds(g * 256, 256)], n_rows.at[slot]

    def turn(g):
        src, dst = turned(g)
        return remote(src, dst, turn_send.at[g], turn_recv.at[core], at(y_lo, x, g, y_hi, z))

    def turn_here(g):
        src, dst = turned(g)
        return pltpu.make_async_copy(src, dst, turn_recv.at[core])

    for turn_index in range(2):
        for i in range(3):
            n_copy(i, turn_index).wait_recv()
        total = n_part[3, turn_index] + n_got[0, turn_index] + n_got[1, turn_index] + n_got[2, turn_index]
        for g in range(2):

            @pl.when((core + turn_index) % 2 == g)
            def _():
                n_ref[:, g * 256 : (g + 1) * 256] = total

                @pl.when(jnp.logical_and(stays, core == g))
                def _():
                    turn_here(g).start()

                @pl.when(jnp.logical_not(jnp.logical_and(stays, core == g)))
                def _():
                    turn(g).start()

    def side(g):
        rows = n_rows.at[pl.ds(pl.multiple_of((y_lo * 2 + g) * 448, 64), 448)]
        return remote(rows, rows, side_send.at[g], side_recv.at[g], (row_partner, col))

    for g in range(2):
        rows = n_rows.at[pl.ds(pl.multiple_of((y_lo * 2 + g) * 448, 64), 448)]
        pltpu.make_async_copy(rows, rows, turn_recv.at[g]).wait()
        side(g).start()
    for g in range(2):
        side(g).wait_recv()

    for k in range(7):
        rows = slice(k * 256, (k + 1) * 256)
        t_high[:, rows], t_low[:, rows] = split(n_rows[rows, :].T)

    def d_copy(i):
        to = (x + i + 1) % 4
        return remote(d_part.at[i], d_got.at[i], d_send.at[i], d_recv.at[i], (y_lo * 4 + to, col))

    @pl.loop(0, 4)
    def _(i):
        block = (x + i + 1) % 4
        for half in range(2):
            d_part[i, :, half * 256 : (half + 1) * 256] = three(
                t_high[...], t_low[...], p_high[block, half], p_low[block, half]
            )

        @pl.when(i < 3)
        def _():
            d_copy(i).start()

    for i in range(3):
        d_copy(i).wait_recv()
    d_ref[...] = d_part[3] + d_got[0] + d_got[1] + d_got[2]

    @pl.loop(1, 16)
    def _(k):
        first(k).wait_send()

    @pl.loop(1, 4)
    def _(k):
        second(k).wait_send()

    k_copy.wait_send()

    @pl.loop(0, 4)
    def _(i):
        for kind in range(10):
            gather(kind, i).wait_send()

    @pl.loop(0, 3)
    def _(i):
        for turn_index in range(2):
            n_copy(i, turn_index).wait_send()
        d_copy(i).wait_send()

    for g in range(2):
        side(g).wait_send()

        @pl.when(jnp.logical_not(jnp.logical_and(stays, core == g)))
        def _():
            turn(g).wait_send()


def on_device(known_inverse, factor_panel, diag_base, ancestor_map):
    blocks = jnp.arange(28, dtype=jnp.int32)
    inverse = jnp.sum(jnp.where(ancestor_map[None, :] == blocks[:, None], blocks[None, :], 0), axis=1)
    vmem = pl.BlockSpec(memory_space=pltpu.VMEM)
    dma = pltpu.SemaphoreType.DMA
    product, reduced = pl.pallas_call(
        kernel,
        out_shape=(jax.ShapeDtypeStruct((448, 512), F32), jax.ShapeDtypeStruct((256, 512), F32)),
        in_specs=[pl.BlockSpec(memory_space=pltpu.SMEM), vmem, vmem],
        out_specs=(vmem, vmem),
        scratch_shapes=[
            pltpu.VMEM((448, 896), F32),
            pltpu.VMEM((448, 1792), BF),
            pltpu.VMEM((448, 1792), BF),
            pltpu.VMEM((112, 8, 256), F32),
            pltpu.VMEM((4, 28, 8, 256), F32),
            pltpu.VMEM((4, 2, 28, 64, 256), F32),
            pltpu.VMEM((4, 2, 1792, 256), BF),
            pltpu.VMEM((4, 2, 1792, 256), BF),
            pltpu.VMEM((4, 2, 448, 256), F32),
            pltpu.VMEM((3, 2, 448, 256), F32),
            pltpu.VMEM((1792, 256), F32),
            pltpu.VMEM((256, 1792), BF),
            pltpu.VMEM((256, 1792), BF),
            pltpu.VMEM((4, 256, 512), F32),
            pltpu.VMEM((3, 256, 512), F32),
            dma((2,)), dma((16,)), dma((16,)), dma((4,)), dma((4,)), dma((10, 4)), dma((10, 4)),
            dma((3, 2)), dma((3, 2)), dma((2,)), dma((2,)), dma((2,)), dma((2,)), dma((3,)), dma((3,)), dma((2,)),
        ],
        compiler_params=pltpu.CompilerParams(collective_id=0, has_side_effects=True, vmem_limit_bytes=60 << 20),
        cost_estimate=pl.CostEstimate(flops=3 * 2 * (448 * 1792 * 2048 + 256 * 1792 * 2048), bytes_accessed=4 << 20, transcendentals=0),
        name="selected_inverse",
    )(inverse, known_inverse, factor_panel.reshape(7, 8, 8, 512))
    return (-product, diag_base + reduced.T)


def solution(mesh):
    placed = (P("col", "row"), P("col", "row"), P("row", "col"), P())
    return jax.shard_map(
        on_device,
        mesh=mesh,
        in_specs=placed,
        out_specs=(P("col", "row"), P("row", "col")),
        check_vma=False,
    )
```

time: 480 us -> 247 us (0.51)
  waiting for transfers between devices: 394 us -> 0 us
  Pallas kernels: 0 us -> 238 us
  matrix products: 43.2 us -> 0 us
  local copies, waits for them, and re-layouts: 15 us -> 1.2 us
  between operations: 13.8 us -> 0.67 us
  other arithmetic: 13.4 us -> 3.47 us
    all_gather x3 -> x0, waiting for transfers between devices: 292 us -> none  [the longest x1 108 us: on_device(): lax.all_gather(known_inverse, 'row', axis=1, tiled=True)]
    pallas_call x0 -> x1, Pallas kernels: none -> 238 us  [on_device(): pl.pallas_call(kernel, out_shape=(jax.ShapeDtypeStruct((448, 512), F32),...]
    reduce_scatter x1 -> x0, waiting for transfers between devices: 100 us -> none  [on_device(): lax.psum_scatter(lax.dot_general(spread_rows, own_rows, (((0,), (0,)), ((...]
    dot_general x2 -> x0, matrix products: 43.2 us -> none  [the longest x1 25.3 us: on_device(): jnp.dot(lax.all_gather(known_inverse, 'row', axis=1, tiled=True), placed,...]
    gather x1 -> x0, local copies, waits for them, and re-layouts: 13.1 us -> none  [on_device(): jnp.take(panel.reshape(block_count, block_rows, panel.shape[1]), inverse,...]
    select_n x3 -> x0, other arithmetic: 12.2 us -> none  [the longest x2 11.6 us: on_device(): jnp.take(panel.reshape(block_count, block_rows, panel.shape[1]), inverse,...]
  transfers between devices with their start and end apart: 4 -> 0, of which waited for: 4 -> 0; matrix products, arithmetic and copies ran while one was open for 5% -> 0% of each run, Pallas kernels for 0% -> 0%
where the time goes in v1:
time: 247 us; the launch traced here: 243 us
  Pallas kernels  238 us (96%)
  other arithmetic  3.47 us (1%)
    pallas_call x1, Pallas kernels, on_device(): pl.pallas_call(kernel, out_shape=(jax.ShapeDtypeStruct((448, 512), F32),...  238 us

profile of v1, /device:TPU:1, one launch (start us, length us, event | category | flops | bytes accessed | tf_op | source)
XLA Modules:
  0.0 242.9 jit_solution(11114200282378144741)
XLA Ops:
  0.6 1.3 select_reduce_fusion.inv_ref
  1.9 0.0 copy-start.1
  1.9 237.5 %selected_inverse.1 = (f32[448,512]{1,0:T(8,128)}, f32[256,512]{1,0:T(8,128)}) custom-call(s32[28]{0:T(128)} %select_reduce_fusion.inv_ref, f32[448,896]{1,0:T(8,128)} %k_ref.1, f32[7,8,8,512]{3,2,1,0:T(8,128)} %bitcast.3), custom_call_target="tpu_custom_call" | custom-call | flops 15502147584 | bytes 4194304 | tf_op jit(solution)/shard_map/selected_inverse/pallas_call | solution.py:319
  239.5 0.0 copy-done.1
  239.5 0.0 copy-start
  239.5 0.2 copy.8
  239.7 1.2 bitcast_add_fusion
  240.9 1.0 copy.9
  241.9 0.0 copy-done
  241.9 1.0 neg.3
Async XLA Ops:
  1.9 237.6 %copy-start.1 = (f32[512,256]{1,0:T(8,128)S(1)}, f32[512,256]{1,0:T(8,128)}, u32[]{:S(2)}) copy-start(f32[512,256]{1,0:T(8,128)} %param.6) | copy-start | bytes 1572868
  239.5 2.4 copy-start

commit v2 on v0

v2 whole, which is shorter than its diff:
```python
import jax
import jax.numpy as jnp
from jax import lax
from jax.experimental import pallas as pl
from jax.experimental.pallas import tpu as pltpu
from jax.sharding import PartitionSpec as P

MESH = pl.DeviceIdType.MESH
BF = jnp.bfloat16
F32 = jnp.float32

UP, DOWN, HALF_UP, HALF_DOWN, CORE = range(5)


def split(value):
    high = value.astype(BF)
    return high, (value - high.astype(F32)).astype(BF)


def three(a_high, a_low, b_high, b_low):
    def dot(a, b):
        return jnp.dot(a, b, preferred_element_type=F32)

    return dot(a_high, b_high) + (dot(a_high, b_low) + dot(a_low, b_high))


def kernel(
    inv_ref, k_ref, f_ref, n_ref, d_ref,
    k_all, k_high, k_low, sent_0, sent_1, picked, p_x, p_high, p_low, p_z, pz_high, pz_low,
    n_part, n_got, n_all, t_high, t_low, d_part, d_core, d_got, d_sum, d_out,
    one_send, one_recv, two_send, two_recv, three_send, three_recv, local_sem, k_send, k_recv,
    z_send, z_recv, x_send, x_recv, n_send, n_recv, y_send, y_recv,
    c_send, c_recv, d_send, d_recv, o_send, o_recv,
):
    row, col = lax.axis_index("row"), lax.axis_index("col")
    x, y_lo = row % 4, row // 4
    core, z, y_hi = col % 2, (col // 2) % 4, col // 8
    y, place = y_hi * 2 + y_lo, col % 8

    def at(y_hi_, z_, core_, y_lo_, x_):
        return (y_lo_ * 4 + x_, y_hi_ * 8 + z_ * 2 + core_)

    def on_x(k):
        return (y_lo * 4 + (x + k) % 4, col)

    def on_y(k):
        there = (y + k) % 4
        return at(there // 2, z, core, there % 2, x)

    def on_z(k):
        return (row, y_hi * 8 + ((z + k) % 4) * 2 + core)

    other_core = (row, y_hi * 8 + z * 2 + 1 - core)
    stays = jnp.logical_and(y_hi == y_lo, y_hi == core)

    def remote(src, dst, send, recv, device):
        return pltpu.make_async_remote_copy(
            src_ref=src, dst_ref=dst, send_sem=send, recv_sem=recv, device_id=device, device_id_type=MESH
        )

    barrier = pltpu.get_barrier_semaphore()

    def greet(device):
        pl.semaphore_signal(barrier, inc=1, device_id=device, device_id_type=MESH)

    @pl.loop(1, 16)
    def _(k):
        greet((row, (col + k) % 16))

    for k in (1, 2, 3):
        greet(on_x(k))
    for k in (1, 3):
        greet(on_y(k))

    @pl.when(jnp.logical_not(stays))
    def _():
        greet(at(core, z, y_lo, y_hi, x))

    pl.semaphore_wait(barrier, 21 - stays.astype(jnp.int32))

    sent = (sent_0, sent_1)

    def piece(to, e):
        return f_ref.at[:, to % 8, :, pl.ds(pl.multiple_of((to // 8) * 256 + e * 128, 128), 128)]

    def first(e, k):
        to = (col + k) % 16
        return remote(piece(to, e), sent[e].at[pl.ds(col * 7, 7)], one_send.at[e, k], one_recv.at[e, k], (row, to))

    def first_here(e):
        return pltpu.make_async_copy(piece(col, e), sent[e].at[pl.ds(col * 7, 7)], local_sem.at[e])

    for e in range(2):

        @pl.loop(1, 16)
        def _(k):
            first(e, k).start()

        first_here(e).start()

    def k_copy(kind, half):
        rows = pl.ds(half * 224, 224)
        return remote(
            k_ref.at[rows], k_all.at[y, rows], k_send.at[kind, half], k_recv.at[kind, half], on_y(1 if kind == UP else 3)
        )

    def k_pass(kind):
        rows = pl.ds(0, 224) if kind == HALF_UP else pl.ds(224, 224)
        ref = k_all.at[(y + (3 if kind == HALF_UP else 1)) % 4, rows]
        return remote(ref, ref, k_send.at[kind, 0], k_recv.at[kind, 0], on_y(1 if kind == HALF_UP else 3))

    k_copy(UP, 0).start()
    k_copy(DOWN, 1).start()
    k_copy(UP, 1).start()
    k_copy(DOWN, 0).start()

    def take_k(there, ref):
        for side in range(2):

            @pl.when(there % 2 == side)
            def _():
                columns = slice(side * 896, (side + 1) * 896)
                k_high[there // 2, :, columns], k_low[there // 2, :, columns] = split(ref[...])

    take_k(y, k_ref)

    def second(e, k):
        to = (x + 4 - k) % 4
        i = (k + 3) % 4
        src = picked.at[e, :, pl.ds(to * 14, 14)]
        dst = p_x.at[e, i // 2, i % 2, :, :, z, core]
        if k == 0:
            return pltpu.make_async_copy(src, dst, local_sem.at[2 + e])
        return remote(src, dst, two_send.at[e, k], two_recv.at[e, k], on_x(4 - k))

    def third(e, k):
        to = (place + k) % 8
        src = picked.at[e, :, pl.ds(to * 7, 7)]
        dst = p_z.at[e, x, :, :, place]
        return remote(src, dst, three_send.at[e, k], three_recv.at[e, k], (row, y_hi * 8 + to))

    def third_here(e):
        src = picked.at[e, :, pl.ds(place * 7, 7)]
        return pltpu.make_async_copy(src, p_z.at[e, x, :, :, place], local_sem.at[4 + e])

    for e in range(2):
        first_here(e).wait()

        @pl.loop(1, 16)
        def _(k):
            first(e, k).wait_recv()

        for j in range(28):
            picked[e, j // 14, (j % 14) * 4 : (j % 14) * 4 + 4] = sent[e][pl.ds(inv_ref[j] * 4, 4)]
        for k in (1, 2, 3, 0):
            second(e, k).start()

        @pl.loop(1, 8)
        def _(k):
            third(e, k).start()

        third_here(e).start()

    def z_copy(kind, r):
        def rows(there, chunk=slice(None)):
            return p_x.at[r // 2, r % 2, :, chunk, :, there, core]

        if kind == CORE:
            ref, to = p_x.at[r // 2, r % 2, :, :, :, :, core], other_core
        else:
            ref, to = {
                UP: (rows(z), on_z(1)),
                DOWN: (rows(z), on_z(3)),
                HALF_UP: (rows((z + 3) % 4, 0), on_z(1)),
                HALF_DOWN: (rows((z + 1) % 4, 1), on_z(3)),
            }[kind]
        return remote(ref, ref, z_send.at[kind, r], z_recv.at[kind, r], to)

    def x_copy(kind, e):
        def block(there, half=slice(None)):
            return p_z.at[e, there, half]

        ref, to = {
            UP: (block(x), on_x(1)),
            DOWN: (block(x), on_x(3)),
            HALF_UP: (block((x + 3) % 4, 0), on_x(1)),
            HALF_DOWN: (block((x + 1) % 4, 1), on_x(3)),
        }[kind]
        return remote(ref, ref, x_send.at[kind, e], x_recv.at[kind, e], to)

    def pass_on(copy, r):
        copy(UP, r).wait_recv()
        copy(HALF_UP, r).start()
        copy(DOWN, r).wait_recv()
        copy(HALF_DOWN, r).start()

    def third_done(e):
        third_here(e).wait()

        @pl.loop(1, 8)
        def _(k):
            third(e, k).wait_recv()

    for e in range(2):
        second(e, 0).wait()
        for k in (1, 2, 3):
            second(e, k).wait_recv()
        for p in range(2):
            z_copy(UP, 2 * e + p).start()
            z_copy(DOWN, 2 * e + p).start()
        third_done(e)
        if e == 0:
            x_copy(UP, 0).start()
            x_copy(DOWN, 0).start()

    k_copy(UP, 0).wait_recv()
    k_pass(HALF_UP).start()
    k_copy(DOWN, 1).wait_recv()
    k_pass(HALF_DOWN).start()

    def core_start(r):
        z_copy(HALF_UP, r).wait_recv()
        z_copy(HALF_DOWN, r).wait_recv()
        z_copy(CORE, r).start()

    pass_on(z_copy, 0)
    pass_on(z_copy, 1)
    core_start(0)
    k_copy(UP, 1).wait_recv()
    k_copy(DOWN, 0).wait_recv()
    take_k((y + 3) % 4, k_all.at[(y + 3) % 4])
    take_k((y + 1) % 4, k_all.at[(y + 1) % 4])
    pass_on(x_copy, 0)

    def n_copy(e, i, side):
        src = n_part.at[2 * e + i // 2, side, :, pl.ds((i % 2) * 128, 128)]
        return remote(src, n_got.at[i, e, side], n_send.at[i, e, side], n_recv.at[i, e, side], on_x(i + 1))

    def n_unit(r, side):
        e, p = r // 2, r % 2

        @pl.loop(0, 14)
        def _(k):
            for half in range(2):
                rows = pl.ds(pl.multiple_of(half * 896 + k * 64, 64), 64)
                for i in range(2):
                    columns = slice(i * 128, (i + 1) * 128)
                    p_high[rows, columns], p_low[rows, columns] = split(p_x[e, p, i, half, k].reshape(64, 128))

        n_part[r, side] = three(k_high[side], k_low[side], p_high[...], p_low[...])

        @pl.when(p == 0)
        def _():
            n_copy(e, 0, side).start()
            n_copy(e, 1, side).start()

        @pl.when(p == 1)
        def _():
            n_copy(e, 2, side).start()

    @pl.loop(0, 4)
    def _(r):
        @pl.when(r < 2)
        def _():
            pass_on(z_copy, r + 2)

        @pl.when(r < 3)
        def _():
            core_start(r + 1)

        z_copy(CORE, r).wait_recv()
        n_unit(r, y_hi)

    k_pass(HALF_UP).wait_recv()
    k_pass(HALF_DOWN).wait_recv()
    take_k((y + 2) % 4, k_all.at[(y + 2) % 4])

    @pl.loop(0, 4)
    def _(r):
        n_unit(r, 1 - y_hi)

    x_copy(UP, 1).start()
    x_copy(DOWN, 1).start()

    def y_copy(e, k):
        ref = n_all.at[e, y]
        return remote(ref, ref, y_send.at[e, k], y_recv.at[e, k], on_y(k))

    for e in range(2):
        for side in range(2):
            for i in range(3):
                n_copy(e, i, side).wait_recv()
            n_all[e, y, side * 448 : (side + 1) * 448] = n_part[2 * e + 1, side, :, 128:256] + (
                n_got[0, e, side] + n_got[1, e, side] + n_got[2, e, side]
            )
        for k in (1, 3, 2):
            y_copy(e, k).start()
        if e == 0:
            pass_on(x_copy, 1)

    for e in range(2):
        x_copy(HALF_UP, e).wait_recv()
        x_copy(HALF_DOWN, e).wait_recv()

    @pl.loop(0, 4)
    def _(there):
        for half in range(2):
            rows = slice(half * 448, (half + 1) * 448)
            for e in range(2):
                columns = slice(e * 128, (e + 1) * 128)
                pz_high[there, rows, columns], pz_low[there, rows, columns] = split(p_z[e, there, half].reshape(448, 128))

    def c_copy(e):
        return remote(d_part.at[e, 1 - core], d_core.at[e], c_send.at[e], c_recv.at[e], other_core)

    def d_copy(e, k):
        return remote(d_part.at[e, core, (z + k) % 4], d_got.at[e, k - 1], d_send.at[e, k - 1], d_recv.at[e, k - 1], on_z(k))

    @pl.loop(0, 2)
    def _(e):
        for k in (1, 3, 2):
            y_copy(e, k).wait_recv()
        for low in range(2):
            for high in range(2):
                for k in range(7):
                    rows = slice(k * 128, (k + 1) * 128)
                    lines = slice(high * 128, (high + 1) * 128)
                    t_high[low, lines, rows], t_low[low, lines, rows] = split(n_all[e, 2 * high + low, rows].T)

        @pl.loop(0, 2)
        def _(turn):
            low = (core + 1 + turn) % 2

            @pl.loop(0, 4)
            def _(there):
                d_part[e, low, there] = three(t_high[low], t_low[low], pz_high[there], pz_low[there])

            @pl.when(turn == 0)
            def _():
                c_copy(e).start()

        c_copy(e).wait_recv()

        @pl.loop(0, 4)
        def _(there):
            d_part[e, core, there] += d_core[e, there]

        for k in (1, 3, 2):
            d_copy(e, k).start()

    def o_copy(e):
        return remote(d_sum.at[e], d_out.at[e], o_send.at[e], o_recv.at[e], at(y_lo, z, y_hi, core, x))

    for e in range(2):
        for k in (1, 3, 2):
            d_copy(e, k).wait_recv()
        d_sum[e] = d_part[e, core, z] + (d_got[e, 0] + d_got[e, 1] + d_got[e, 2])

        @pl.when(stays)
        def _():
            pltpu.make_async_copy(d_sum.at[e], d_out.at[e], o_recv.at[e]).start()

        @pl.when(jnp.logical_not(stays))
        def _():
            o_copy(e).start()

    for e in range(2):
        for half in range(2):
            n_ref[:, half * 256 + e * 128 : half * 256 + (e + 1) * 128] = n_all[
                e, half * 2 + y_lo, pl.ds(pl.multiple_of(y_hi * 448, 64), 448)
            ]

    for e in range(2):
        pltpu.make_async_copy(d_sum.at[e], d_out.at[e], o_recv.at[e]).wait()
        d_ref[0, e] = d_out[e, 0:128]
        d_ref[1, e] = d_out[e, 128:256]

    for e in range(2):

        @pl.loop(1, 16)
        def _(k):
            first(e, k).wait_send()

        @pl.loop(1, 8)
        def _(k):
            third(e, k).wait_send()

        for k in (1, 2, 3):
            second(e, k).wait_send()
            y_copy(e, k).wait_send()
            d_copy(e, k).wait_send()
        for kind in range(4):
            x_copy(kind, e).wait_send()
        for i in range(3):
            for side in range(2):
                n_copy(e, i, side).wait_send()
        c_copy(e).wait_send()

        @pl.when(jnp.logical_not(stays))
        def _():
            o_copy(e).wait_send()

    for half in range(2):
        k_copy(UP, half).wait_send()
        k_copy(DOWN, half).wait_send()
    k_pass(HALF_UP).wait_send()
    k_pass(HALF_DOWN).wait_send()

    @pl.loop(0, 4)
    def _(r):
        for kind in range(5):
            z_copy(kind, r).wait_send()


def on_device(known_inverse, factor_panel, diag_base, ancestor_map):
    blocks = jnp.arange(28, dtype=jnp.int32)
    inverse = jnp.sum(jnp.where(ancestor_map[None, :] == blocks[:, None], blocks[None, :], 0), axis=1)
    vmem = pl.BlockSpec(memory_space=pltpu.VMEM)
    dma = pltpu.SemaphoreType.DMA
    product, reduced = pl.pallas_call(
        kernel,
        out_shape=(jax.ShapeDtypeStruct((448, 512), F32), jax.ShapeDtypeStruct((2, 2, 128, 256), F32)),
        in_specs=[pl.BlockSpec(memory_space=pltpu.SMEM), vmem, vmem],
        out_specs=(vmem, vmem),
        scratch_shapes=[
            pltpu.VMEM((4, 448, 896), F32),
            pltpu.VMEM((2, 448, 1792), BF),
            pltpu.VMEM((2, 448, 1792), BF),
            pltpu.VMEM((112, 8, 128), F32),
            pltpu.VMEM((112, 8, 128), F32),
            pltpu.VMEM((2, 2, 56, 8, 128), F32),
            pltpu.VMEM((2, 2, 2, 2, 14, 4, 2, 8, 128), F32),
            pltpu.VMEM((1792, 256), BF),
            pltpu.VMEM((1792, 256), BF),
            pltpu.VMEM((2, 4, 2, 7, 8, 8, 128), F32),
            pltpu.VMEM((4, 896, 256), BF),
            pltpu.VMEM((4, 896, 256), BF),
            pltpu.VMEM((4, 2, 448, 256), F32),
            pltpu.VMEM((3, 2, 2, 448, 128), F32),
            pltpu.VMEM((2, 4, 896, 128), F32),
            pltpu.VMEM((2, 256, 896), BF),
            pltpu.VMEM((2, 256, 896), BF),
            pltpu.VMEM((2, 2, 4, 256, 256), F32),
            pltpu.VMEM((2, 4, 256, 256), F32),
            pltpu.VMEM((2, 3, 256, 256), F32),
            pltpu.VMEM((2, 256, 256), F32),
            pltpu.VMEM((2, 256, 256), F32),
            dma((2, 16)), dma((2, 16)), dma((2, 4)), dma((2, 4)), dma((2, 8)), dma((2, 8)), dma((6,)), dma((4, 2)), dma((4, 2)),
            dma((5, 4)), dma((5, 4)), dma((4, 2)), dma((4, 2)), dma((3, 2, 2)), dma((3, 2, 2)), dma((2, 4)), dma((2, 4)),
            dma((2,)), dma((2,)), dma((2, 3)), dma((2, 3)), dma((2,)), dma((2,)),
        ],
        compiler_params=pltpu.CompilerParams(collective_id=0, has_side_effects=True, vmem_limit_bytes=60 << 20),
        cost_estimate=pl.CostEstimate(
            flops=6 * (448 * 1792 * 2048 + 256 * 1792 * 2048), bytes_accessed=4 << 20, transcendentals=0
        ),
        name="selected_inverse",
    )(inverse, known_inverse, factor_panel.reshape(7, 8, 8, 512))
    return (-product, diag_base + reduced.reshape(512, 256))


def solution(mesh):
    placed = (P("col", "row"), P("col", "row"), P("row", "col"), P())
    return jax.shard_map(
        on_device,
        mesh=mesh,
        in_specs=placed,
        out_specs=(P("col", "row"), P("row", "col")),
        check_vma=False,
    )
```

time: 480 us -> 169 us (0.35)
  waiting for transfers between devices: 394 us -> 0 us
  Pallas kernels: 0 us -> 164 us
  matrix products: 43.2 us -> 0 us
  local copies, waits for them, and re-layouts: 15 us -> 0.01 us
  between operations: 13.8 us -> 0.66 us
  other arithmetic: 13.4 us -> 4.41 us
    all_gather x3 -> x0, waiting for transfers between devices: 292 us -> none  [the longest x1 108 us: on_device(): lax.all_gather(known_inverse, 'row', axis=1, tiled=True)]
    pallas_call x0 -> x1, Pallas kernels: none -> 164 us  [on_device(): pl.pallas_call(kernel, out_shape=(jax.ShapeDtypeStruct((448, 512), F32),...]
    reduce_scatter x1 -> x0, waiting for transfers between devices: 100 us -> none  [on_device(): lax.psum_scatter(lax.dot_general(spread_rows, own_rows, (((0,), (0,)), ((...]
    dot_general x2 -> x0, matrix products: 43.2 us -> none  [the longest x1 25.3 us: on_device(): jnp.dot(lax.all_gather(known_inverse, 'row', axis=1, tiled=True), placed,...]
    gather x1 -> x0, local copies, waits for them, and re-layouts: 13.1 us -> none  [on_device(): jnp.take(panel.reshape(block_count, block_rows, panel.shape[1]), inverse,...]
    select_n x3 -> x0, other arithmetic: 12.2 us -> none  [the longest x2 11.6 us: on_device(): jnp.take(panel.reshape(block_count, block_rows, panel.shape[1]), inverse,...]
  transfers between devices with their start and end apart: 4 -> 0, of which waited for: 4 -> 0; matrix products, arithmetic and copies ran while one was open for 5% -> 0% of each run, Pallas kernels for 0% -> 0%
where the time goes in v2:
time: 169 us
  Pallas kernels  164 us (97%)
  other arithmetic  4.41 us (3%)
    pallas_call x1, Pallas kernels, on_device(): pl.pallas_call(kernel, out_shape=(jax.ShapeDtypeStruct((448, 512), F32),...  164 us

profile of v2, /device:TPU:1, one launch (start us, length us, event | category | flops | bytes accessed | tf_op | source)
XLA Modules:
  0.0 169.3 jit_solution(6891433949000827301)
XLA Ops:
  0.6 1.3 select_reduce_fusion.inv_ref
  1.9 164.2 %selected_inverse.1 = (f32[448,512]{1,0:T(8,128)}, f32[2,2,128,256]{3,2,1,0:T(8,128)}) custom-call(s32[28]{0:T(128)} %select_reduce_fusion.inv_ref, f32[448,896]{1,0:T(8,128)} %k_ref.1, f32[7,8,8,512]{3,2,1,0:T(8,128)} %bitcast.3), custom_call_target="tpu_custom_call" | custom-call | flops 15502147584 | bytes 4194304 | tf_op jit(solution)/shard_map/selected_inverse/pallas_call | solution.py:420
  166.1 0.0 copy-start
  166.2 0.0 copy-start.1
  166.2 2.3 %neg.3 = f32[448,512]{1,0:T(8,128)} negate(f32[448,512]{1,0:T(8,128)} %get-tuple-element.4) | non-fusion elementwise | flops 229376 | bytes 1835008 | tf_op jit(solution)/shard_map/neg | solution.py:458
  168.4 0.0 copy-done
  168.4 0.0 copy-done.1
  168.4 0.9 bitcast_add_fusion
Async XLA Ops:
  166.1 2.3 %copy-start = (f32[512,256]{1,0:T(8,128)S(1)}, f32[512,256]{1,0:T(8,128)}, u32[]{:S(2)}) copy-start(f32[512,256]{1,0:T(8,128)} %param.6) | copy-start | bytes 1572868
  166.2 2.3 %copy-start.1 = (f32[2,2,128,256]{3,2,1,0:T(8,128)S(1)}, f32[2,2,128,256]{3,2,1,0:T(8,128)}, u32[]{:S(2)}) copy-start(f32[2,2,128,256]{3,2,1,0:T(8,128)} %get-tuple-element.5) | copy-start | bytes 1572868

commit v3 on v2

--- a/solution.py
+++ b/solution.py
@@ -27,7 +27,7 @@
 def kernel(
     inv_ref, k_ref, f_ref, n_ref, d_ref,
     k_all, k_high, k_low, sent_0, sent_1, picked, p_x, p_high, p_low, p_z, pz_high, pz_low,
-    n_part, n_got, n_all, t_high, t_low, d_part, d_core, d_got, d_sum, d_out,
+    n_part, n_far, n_got, n_all, t_high, t_low, d_part, d_core, d_got, d_sum, d_out,
     one_send, one_recv, two_send, two_recv, three_send, three_recv, local_sem, k_send, k_recv,
     z_send, z_recv, x_send, x_recv, n_send, n_recv, y_send, y_recv,
     c_send, c_recv, d_send, d_recv, o_send, o_recv,
@@ -111,16 +111,9 @@
 
     k_copy(UP, 0).start()
     k_copy(DOWN, 1).start()
-    k_copy(UP, 1).start()
-    k_copy(DOWN, 0).start()
 
     def take_k(there, ref):
-        for side in range(2):
-
-            @pl.when(there % 2 == side)
-            def _():
-                columns = slice(side * 896, (side + 1) * 896)
-                k_high[there // 2, :, columns], k_low[there // 2, :, columns] = split(ref[...])
+        k_high[there], k_low[there] = split(ref[...])
 
     take_k(y, k_ref)
 
@@ -160,6 +153,9 @@
             third(e, k).start()
 
         third_here(e).start()
+        if e == 0:
+            k_copy(UP, 1).start()
+            k_copy(DOWN, 0).start()
 
     def z_copy(kind, r):
         def rows(there, chunk=slice(None)):
@@ -209,14 +205,13 @@
             z_copy(UP, 2 * e + p).start()
             z_copy(DOWN, 2 * e + p).start()
         third_done(e)
+        x_copy(UP, e).start()
+        x_copy(DOWN, e).start()
         if e == 0:
-            x_copy(UP, 0).start()
-            x_copy(DOWN, 0).start()
-
-    k_copy(UP, 0).wait_recv()
-    k_pass(HALF_UP).start()
-    k_copy(DOWN, 1).wait_recv()
-    k_pass(HALF_DOWN).start()
+            k_copy(UP, 0).wait_recv()
+            k_pass(HALF_UP).start()
+            k_copy(DOWN, 1).wait_recv()
+            k_pass(HALF_DOWN).start()
 
     def core_start(r):
         z_copy(HALF_UP, r).wait_recv()
@@ -226,77 +221,116 @@
     pass_on(z_copy, 0)
     pass_on(z_copy, 1)
     core_start(0)
+    pass_on(z_copy, 2)
+    core_start(1)
+    pass_on(x_copy, 0)
+    pass_on(z_copy, 3)
     k_copy(UP, 1).wait_recv()
     k_copy(DOWN, 0).wait_recv()
     take_k((y + 3) % 4, k_all.at[(y + 3) % 4])
     take_k((y + 1) % 4, k_all.at[(y + 1) % 4])
-    pass_on(x_copy, 0)
-
-    def n_copy(e, i, side):
-        src = n_part.at[2 * e + i // 2, side, :, pl.ds((i % 2) * 128, 128)]
-        return remote(src, n_got.at[i, e, side], n_send.at[i, e, side], n_recv.at[i, e, side], on_x(i + 1))
-
-    def n_unit(r, side):
-        e, p = r // 2, r % 2
-
-        @pl.loop(0, 14)
-        def _(k):
-            for half in range(2):
-                rows = pl.ds(pl.multiple_of(half * 896 + k * 64, 64), 64)
-                for i in range(2):
-                    columns = slice(i * 128, (i + 1) * 128)
-                    p_high[rows, columns], p_low[rows, columns] = split(p_x[e, p, i, half, k].reshape(64, 128))
-
-        n_part[r, side] = three(k_high[side], k_low[side], p_high[...], p_low[...])
-
-        @pl.when(p == 0)
-        def _():
-            n_copy(e, 0, side).start()
-            n_copy(e, 1, side).start()
-
-        @pl.when(p == 1)
-        def _():
-            n_copy(e, 2, side).start()
+    pass_on(x_copy, 1)
+
+    def n_copy(kind, e, side):
+        src, dst = {
+            HALF_UP: (n_part.at[e, 1, side, pl.ds(0, 224)], n_far.at[0, e, side]),
+            HALF_DOWN: (n_part.at[e, 1, side, pl.ds(224, 224)], n_far.at[1, e, side]),
+            UP: (n_part.at[e, 0, side], n_got.at[0, e, side]),
+            DOWN: (n_part.at[e, 2, side], n_got.at[1, e, side]),
+        }[kind]
+        to = on_x(1 if kind in (UP, HALF_UP) else 3)
+        return remote(src, dst, n_send.at[kind, e, side], n_recv.at[kind, e, side], to)
+
+    def n_passed(r, side):
+        e = r // 2
+
+        @pl.when(r % 2 == 0)
+        def _():
+            n_copy(HALF_UP, e, side).start()
+            n_copy(HALF_DOWN, e, side).start()
+
+        @pl.when(r % 2 == 1)
+        def _():
+            n_copy(HALF_UP, e, side).wait_recv()
+            n_part[e, 0, side, 0:224] += n_far[0, e, side]
+            n_copy(UP, e, side).start()
+            n_copy(HALF_DOWN, e, side).wait_recv()
+            n_part[e, 2, side, 224:448] += n_far[1, e, side]
+            n_copy(DOWN, e, side).start()
+
+    def take_p(r, half):
+        @pl.loop(0, 7)
+        def _(k):
+            rows = pl.ds(pl.multiple_of(k * 128, 128), 128)
+            for i in range(2):
+                columns = slice(i * 128, (i + 1) * 128)
+                p_high[half, rows, columns], p_low[half, rows, columns] = split(
+                    p_x[r // 2, r % 2, i, half, pl.ds(2 * k, 2)].reshape(128, 128)
+                )
+
+    def n_dots(there, half):
+        return three(k_high[there], k_low[there], p_high[half], p_low[half])
+
+    def n_put(r, side, value, add):
+        for i in range(2):
+            columns = value[:, i * 128 : (i + 1) * 128]
+            n_part[r // 2, 2 * (r % 2) + i, side] = columns + n_part[r // 2, 2 * (r % 2) + i, side] if add else columns
+
+    theirs = 1 - y_hi
 
     @pl.loop(0, 4)
     def _(r):
+        z_copy(CORE, r).wait_recv()
+
         @pl.when(r < 2)
         def _():
-            pass_on(z_copy, r + 2)
-
-        @pl.when(r < 3)
-        def _():
-            core_start(r + 1)
-
-        z_copy(CORE, r).wait_recv()
-        n_unit(r, y_hi)
-
+            core_start(r + 2)
+
+        take_p(r, 0)
+        take_p(r, 1)
+        n_put(r, y_hi, n_dots(y, y_lo) + n_dots(y_hi * 2 + 1 - y_lo, 1 - y_lo), False)
+        n_passed(r, y_hi)
+        n_put(r, theirs, n_dots(theirs * 2 + 1 - y_lo, 1 - y_lo), False)
+
+    def y_copy(kind, e, s):
+        there = (y + {UP: 0, DOWN: 0, HALF_UP: 3, HALF_DOWN: 1}[kind]) % 4
+        start = ((there // 2 + s) % 2) * 448 + (224 if kind == HALF_DOWN else 0)
+        size = 448 if kind in (UP, DOWN) else 224
+        ref = n_all.at[e, there, pl.ds(pl.multiple_of(start, 32), size)]
+        to = on_y(1 if kind in (UP, HALF_UP) else 3)
+        return remote(ref, ref, y_send.at[kind, e, s], y_recv.at[kind, e, s], to)
+
+    def y_start(e, s):
+        side = (y_hi + s) % 2
+        n_copy(UP, e, side).wait_recv()
+        n_copy(DOWN, e, side).wait_recv()
+        rows = pl.ds(pl.multiple_of(side * 448, 64), 448)
+        n_all[e, y, rows] = n_part[e, 3, side] + (n_got[0, e, side] + n_got[1, e, side])
+        y_copy(UP, e, s).start()
+        y_copy(DOWN, e, s).start()
+
+    def y_pass(e, s):
+        y_copy(UP, e, s).wait_recv()
+        y_copy(HALF_UP, e, s).start()
+        y_copy(DOWN, e, s).wait_recv()
+        y_copy(HALF_DOWN, e, s).start()
+
+    y_start(0, 0)
+    y_start(1, 0)
     k_pass(HALF_UP).wait_recv()
     k_pass(HALF_DOWN).wait_recv()
     take_k((y + 2) % 4, k_all.at[(y + 2) % 4])
 
     @pl.loop(0, 4)
     def _(r):
-        n_unit(r, 1 - y_hi)
-
-    x_copy(UP, 1).start()
-    x_copy(DOWN, 1).start()
-
-    def y_copy(e, k):
-        ref = n_all.at[e, y]
-        return remote(ref, ref, y_send.at[e, k], y_recv.at[e, k], on_y(k))
-
-    for e in range(2):
-        for side in range(2):
-            for i in range(3):
-                n_copy(e, i, side).wait_recv()
-            n_all[e, y, side * 448 : (side + 1) * 448] = n_part[2 * e + 1, side, :, 128:256] + (
-                n_got[0, e, side] + n_got[1, e, side] + n_got[2, e, side]
-            )
-        for k in (1, 3, 2):
-            y_copy(e, k).start()
-        if e == 0:
-            pass_on(x_copy, 1)
+        take_p(r, y_lo)
+        n_put(r, theirs, n_dots(theirs * 2 + y_lo, y_lo), True)
+        n_passed(r, theirs)
+
+    y_pass(0, 0)
+    y_start(0, 1)
+    y_pass(1, 0)
+    y_start(1, 1)
 
     for e in range(2):
         x_copy(HALF_UP, e).wait_recv()
@@ -310,16 +344,30 @@
                 columns = slice(e * 128, (e + 1) * 128)
                 pz_high[there, rows, columns], pz_low[there, rows, columns] = split(p_z[e, there, half].reshape(448, 128))
 
-    def c_copy(e):
-        return remote(d_part.at[e, 1 - core], d_core.at[e], c_send.at[e], c_recv.at[e], other_core)
+    y_pass(0, 1)
+    y_pass(1, 1)
+
+    def c_copy(e, k):
+        there = (z + k) % 4
+        return remote(d_part.at[e, 1 - core, there], d_core.at[e, there], c_send.at[e, k], c_recv.at[e, k], other_core)
 
     def d_copy(e, k):
-        return remote(d_part.at[e, core, (z + k) % 4], d_got.at[e, k - 1], d_send.at[e, k - 1], d_recv.at[e, k - 1], on_z(k))
+        return remote(d_part.at[e, core, (z + k) % 4], d_got.at[e, k], d_send.at[e, k], d_recv.at[e, k], on_z(k))
+
+    def over_z(e, k):
+        there = (z + k) % 4
+        c_copy(e, k).wait_recv()
+        d_part[e, core, there] += d_core[e, there]
+
+        @pl.when(k != 0)
+        def _():
+            d_copy(e, k).start()
 
     @pl.loop(0, 2)
     def _(e):
-        for k in (1, 3, 2):
-            y_copy(e, k).wait_recv()
+        for kind in (HALF_UP, HALF_DOWN):
+            for s in range(2):
+                y_copy(kind, e, s).wait_recv()
         for low in range(2):
             for high in range(2):
                 for k in range(7):
@@ -327,26 +375,25 @@
                     lines = slice(high * 128, (high + 1) * 128)
                     t_high[low, lines, rows], t_low[low, lines, rows] = split(n_all[e, 2 * high + low, rows].T)
 
-        @pl.loop(0, 2)
-        def _(turn):
-            low = (core + 1 + turn) % 2
-
-            @pl.loop(0, 4)
-            def _(there):
+        @pl.loop(0, 4)
+        def _(j):
+            k = (j + 1) % 4
+            there = (z + k) % 4
+
+            @pl.loop(0, 2)
+            def _(turn):
+                low = (core + 1 + turn) % 2
                 d_part[e, low, there] = three(t_high[low], t_low[low], pz_high[there], pz_low[there])
 
-            @pl.when(turn == 0)
+                @pl.when(turn == 0)
+                def _():
+                    c_copy(e, k).start()
+
+            @pl.when(j > 0)
             def _():
-                c_copy(e).start()
-
-        c_copy(e).wait_recv()
-
-        @pl.loop(0, 4)
-        def _(there):
-            d_part[e, core, there] += d_core[e, there]
-
-        for k in (1, 3, 2):
-            d_copy(e, k).start()
+                over_z(e, j)
+
+        over_z(e, 0)
 
     def o_copy(e):
         return remote(d_sum.at[e], d_out.at[e], o_send.at[e], o_recv.at[e], at(y_lo, z, y_hi, core, x))
@@ -354,7 +401,7 @@
     for e in range(2):
         for k in (1, 3, 2):
             d_copy(e, k).wait_recv()
-        d_sum[e] = d_part[e, core, z] + (d_got[e, 0] + d_got[e, 1] + d_got[e, 2])
+        d_sum[e] = d_part[e, core, z] + (d_got[e, 1] + d_got[e, 2] + d_got[e, 3])
 
         @pl.when(stays)
         def _():
@@ -387,14 +434,13 @@
 
         for k in (1, 2, 3):
             second(e, k).wait_send()
-            y_copy(e, k).wait_send()
             d_copy(e, k).wait_send()
         for kind in range(4):
             x_copy(kind, e).wait_send()
-        for i in range(3):
+            c_copy(e, kind).wait_send()
             for side in range(2):
-                n_copy(e, i, side).wait_send()
-        c_copy(e).wait_send()
+                n_copy(kind, e, side).wait_send()
+                y_copy(kind, e, side).wait_send()
 
         @pl.when(jnp.logical_not(stays))
         def _():
@@ -424,30 +470,31 @@
         out_specs=(vmem, vmem),
         scratch_shapes=[
             pltpu.VMEM((4, 448, 896), F32),
-            pltpu.VMEM((2, 448, 1792), BF),
-            pltpu.VMEM((2, 448, 1792), BF),
+            pltpu.VMEM((4, 448, 896), BF),
+            pltpu.VMEM((4, 448, 896), BF),
             pltpu.VMEM((112, 8, 128), F32),
             pltpu.VMEM((112, 8, 128), F32),
             pltpu.VMEM((2, 2, 56, 8, 128), F32),
             pltpu.VMEM((2, 2, 2, 2, 14, 4, 2, 8, 128), F32),
-            pltpu.VMEM((1792, 256), BF),
-            pltpu.VMEM((1792, 256), BF),
+            pltpu.VMEM((2, 896, 256), BF),
+            pltpu.VMEM((2, 896, 256), BF),
             pltpu.VMEM((2, 4, 2, 7, 8, 8, 128), F32),
             pltpu.VMEM((4, 896, 256), BF),
             pltpu.VMEM((4, 896, 256), BF),
-            pltpu.VMEM((4, 2, 448, 256), F32),
-            pltpu.VMEM((3, 2, 2, 448, 128), F32),
+            pltpu.VMEM((2, 4, 2, 448, 128), F32),
+            pltpu.VMEM((2, 2, 2, 224, 128), F32),
+            pltpu.VMEM((2, 2, 2, 448, 128), F32),
             pltpu.VMEM((2, 4, 896, 128), F32),
             pltpu.VMEM((2, 256, 896), BF),
             pltpu.VMEM((2, 256, 896), BF),
             pltpu.VMEM((2, 2, 4, 256, 256), F32),
             pltpu.VMEM((2, 4, 256, 256), F32),
-            pltpu.VMEM((2, 3, 256, 256), F32),
+            pltpu.VMEM((2, 4, 256, 256), F32),
             pltpu.VMEM((2, 256, 256), F32),
             pltpu.VMEM((2, 256, 256), F32),
             dma((2, 16)), dma((2, 16)), dma((2, 4)), dma((2, 4)), dma((2, 8)), dma((2, 8)), dma((6,)), dma((4, 2)), dma((4, 2)),
-            dma((5, 4)), dma((5, 4)), dma((4, 2)), dma((4, 2)), dma((3, 2, 2)), dma((3, 2, 2)), dma((2, 4)), dma((2, 4)),
-            dma((2,)), dma((2,)), dma((2, 3)), dma((2, 3)), dma((2,)), dma((2,)),
+            dma((5, 4)), dma((5, 4)), dma((4, 2)), dma((4, 2)), dma((4, 2, 2)), dma((4, 2, 2)), dma((4, 2, 2)), dma((4, 2, 2)),
+            dma((2, 4)), dma((2, 4)), dma((2, 4)), dma((2, 4)), dma((2,)), dma((2,)),
         ],
         compiler_params=pltpu.CompilerParams(collective_id=0, has_side_effects=True, vmem_limit_bytes=60 << 20),
         cost_estimate=pl.CostEstimate(

time: 169 us -> 162 us (0.959)
  Pallas kernels: 164 us -> 157 us
    pallas_call x1, Pallas kernels: 164 us -> 157 us  [on_device(): pl.pallas_call(kernel, out_shape=(jax.ShapeDtypeStruct((448, 512), F32),...]
where the time goes in v3:
time: 162 us
  Pallas kernels  157 us (97%)
  other arithmetic  4.41 us (3%)
    pallas_call x1, Pallas kernels, on_device(): pl.pallas_call(kernel, out_shape=(jax.ShapeDtypeStruct((448, 512), F32),...  157 us

profile of v3, /device:TPU:1, one launch (start us, length us, event | category | flops | bytes accessed | tf_op | source)
XLA Modules:
  0.0 162.1 jit_solution(14958195834286086068)
XLA Ops:
  0.6 1.3 select_reduce_fusion.inv_ref
  1.9 157.0 %selected_inverse.1 = (f32[448,512]{1,0:T(8,128)}, f32[2,2,128,256]{3,2,1,0:T(8,128)}) custom-call(s32[28]{0:T(128)} %select_reduce_fusion.inv_ref, f32[448,896]{1,0:T(8,128)} %k_ref.1, f32[7,8,8,512]{3,2,1,0:T(8,128)} %bitcast.3), custom_call_target="tpu_custom_call" | custom-call | flops 15502147584 | bytes 4194304 | tf_op jit(solution)/shard_map/selected_inverse/pallas_call | solution.py:466
  158.9 0.0 copy-start
  158.9 0.0 copy-start.1
  159.0 2.3 %neg.3 = f32[448,512]{1,0:T(8,128)} negate(f32[448,512]{1,0:T(8,128)} %get-tuple-element.4) | non-fusion elementwise | flops 229376 | bytes 1835008 | tf_op jit(solution)/shard_map/neg | solution.py:505
  161.2 0.0 copy-done
  161.2 0.0 copy-done.1
  161.2 0.9 bitcast_add_fusion
Async XLA Ops:
  158.9 2.3 %copy-start = (f32[512,256]{1,0:T(8,128)S(1)}, f32[512,256]{1,0:T(8,128)}, u32[]{:S(2)}) copy-start(f32[512,256]{1,0:T(8,128)} %param.6) | copy-start | bytes 1572868
  158.9 2.3 %copy-start.1 = (f32[2,2,128,256]{3,2,1,0:T(8,128)S(1)}, f32[2,2,128,256]{3,2,1,0:T(8,128)}, u32[]{:S(2)}) copy-start(f32[2,2,128,256]{3,2,1,0:T(8,128)} %get-tuple-element.5) | copy-start | bytes 1572868

commit v4 on v3

--- a/solution.py
+++ b/solution.py
@@ -27,7 +27,7 @@
 def kernel(
     inv_ref, k_ref, f_ref, n_ref, d_ref,
     k_all, k_high, k_low, sent_0, sent_1, picked, p_x, p_high, p_low, p_z, pz_high, pz_low,
-    n_part, n_far, n_got, n_all, t_high, t_low, d_part, d_core, d_got, d_sum, d_out,
+    n_part, n_far, n_got, n_all, t_high, t_low, d_part, d_core, d_far, d_got, d_sum, d_out,
     one_send, one_recv, two_send, two_recv, three_send, three_recv, local_sem, k_send, k_recv,
     z_send, z_recv, x_send, x_recv, n_send, n_recv, y_send, y_recv,
     c_send, c_recv, d_send, d_recv, o_send, o_recv,
@@ -207,11 +207,6 @@
         third_done(e)
         x_copy(UP, e).start()
         x_copy(DOWN, e).start()
-        if e == 0:
-            k_copy(UP, 0).wait_recv()
-            k_pass(HALF_UP).start()
-            k_copy(DOWN, 1).wait_recv()
-            k_pass(HALF_DOWN).start()
 
     def core_start(r):
         z_copy(HALF_UP, r).wait_recv()
@@ -221,12 +216,16 @@
     pass_on(z_copy, 0)
     pass_on(z_copy, 1)
     core_start(0)
+    pass_on(x_copy, 0)
+    core_start(1)
+    for half in range(2):
+        k_copy(UP, half).wait_recv()
+    k_pass(HALF_UP).start()
+    for half in range(2):
+        k_copy(DOWN, half).wait_recv()
+    k_pass(HALF_DOWN).start()
     pass_on(z_copy, 2)
-    core_start(1)
-    pass_on(x_copy, 0)
     pass_on(z_copy, 3)
-    k_copy(UP, 1).wait_recv()
-    k_copy(DOWN, 0).wait_recv()
     take_k((y + 3) % 4, k_all.at[(y + 3) % 4])
     take_k((y + 1) % 4, k_all.at[(y + 1) % 4])
     pass_on(x_copy, 1)
@@ -241,22 +240,17 @@
         to = on_x(1 if kind in (UP, HALF_UP) else 3)
         return remote(src, dst, n_send.at[kind, e, side], n_recv.at[kind, e, side], to)
 
-    def n_passed(r, side):
-        e = r // 2
-
-        @pl.when(r % 2 == 0)
-        def _():
-            n_copy(HALF_UP, e, side).start()
-            n_copy(HALF_DOWN, e, side).start()
-
-        @pl.when(r % 2 == 1)
-        def _():
-            n_copy(HALF_UP, e, side).wait_recv()
-            n_part[e, 0, side, 0:224] += n_far[0, e, side]
-            n_copy(UP, e, side).start()
-            n_copy(HALF_DOWN, e, side).wait_recv()
-            n_part[e, 2, side, 224:448] += n_far[1, e, side]
-            n_copy(DOWN, e, side).start()
+    def n_far_start(e, side):
+        n_copy(HALF_UP, e, side).start()
+        n_copy(HALF_DOWN, e, side).start()
+
+    def n_near_start(e, side):
+        n_copy(HALF_UP, e, side).wait_recv()
+        n_part[e, 0, side, 0:224] += n_far[0, e, side]
+        n_copy(UP, e, side).start()
+        n_copy(HALF_DOWN, e, side).wait_recv()
+        n_part[e, 2, side, 224:448] += n_far[1, e, side]
+        n_copy(DOWN, e, side).start()
 
     def take_p(r, half):
         @pl.loop(0, 7)
@@ -289,8 +283,16 @@
         take_p(r, 0)
         take_p(r, 1)
         n_put(r, y_hi, n_dots(y, y_lo) + n_dots(y_hi * 2 + 1 - y_lo, 1 - y_lo), False)
-        n_passed(r, y_hi)
+
+        @pl.when(r % 2 == 0)
+        def _():
+            n_far_start(r // 2, y_hi)
+
         n_put(r, theirs, n_dots(theirs * 2 + 1 - y_lo, 1 - y_lo), False)
+
+        @pl.when(r % 2 == 1)
+        def _():
+            n_near_start(r // 2, y_hi)
 
     def y_copy(kind, e, s):
         there = (y + {UP: 0, DOWN: 0, HALF_UP: 3, HALF_DOWN: 1}[kind]) % 4
@@ -322,10 +324,18 @@
     take_k((y + 2) % 4, k_all.at[(y + 2) % 4])
 
     @pl.loop(0, 4)
-    def _(r):
+    def _(t):
+        r = (t % 2) * 2 + t // 2
         take_p(r, y_lo)
         n_put(r, theirs, n_dots(theirs * 2 + y_lo, y_lo), True)
-        n_passed(r, theirs)
+
+        @pl.when(t < 2)
+        def _():
+            n_far_start(t, theirs)
+
+        @pl.when(t >= 2)
+        def _():
+            n_near_start(t - 2, theirs)
 
     y_pass(0, 0)
     y_start(0, 1)
@@ -344,27 +354,40 @@
                 columns = slice(e * 128, (e + 1) * 128)
                 pz_high[there, rows, columns], pz_low[there, rows, columns] = split(p_z[e, there, half].reshape(448, 128))
 
-    y_pass(0, 1)
-    y_pass(1, 1)
-
     def c_copy(e, k):
         there = (z + k) % 4
         return remote(d_part.at[e, 1 - core, there], d_core.at[e, there], c_send.at[e, k], c_recv.at[e, k], other_core)
 
-    def d_copy(e, k):
-        return remote(d_part.at[e, core, (z + k) % 4], d_got.at[e, k], d_send.at[e, k], d_recv.at[e, k], on_z(k))
-
-    def over_z(e, k):
+    def d_copy(kind, e):
+        src, dst = {
+            HALF_UP: (d_part.at[e, core, (z + 2) % 4, pl.ds(0, 128)], d_far.at[0, e]),
+            HALF_DOWN: (d_part.at[e, core, (z + 2) % 4, pl.ds(128, 128)], d_far.at[1, e]),
+            UP: (d_part.at[e, core, (z + 1) % 4], d_got.at[0, e]),
+            DOWN: (d_part.at[e, core, (z + 3) % 4], d_got.at[1, e]),
+        }[kind]
+        return remote(src, dst, d_send.at[kind, e], d_recv.at[kind, e], on_z(1 if kind in (UP, HALF_UP) else 3))
+
+    def d_cores(e, k):
         there = (z + k) % 4
         c_copy(e, k).wait_recv()
         d_part[e, core, there] += d_core[e, there]
 
-        @pl.when(k != 0)
-        def _():
-            d_copy(e, k).start()
+    def d_far_start(e):
+        d_cores(e, 2)
+        d_copy(HALF_UP, e).start()
+        d_copy(HALF_DOWN, e).start()
+
+    def d_near_start(e):
+        d_copy(HALF_UP, e).wait_recv()
+        d_part[e, core, (z + 1) % 4, 0:128] += d_far[0, e]
+        d_copy(UP, e).start()
+        d_copy(HALF_DOWN, e).wait_recv()
+        d_part[e, core, (z + 3) % 4, 128:256] += d_far[1, e]
+        d_copy(DOWN, e).start()
 
     @pl.loop(0, 2)
     def _(e):
+        y_pass(e, 1)
         for kind in (HALF_UP, HALF_DOWN):
             for s in range(2):
                 y_copy(kind, e, s).wait_recv()
@@ -377,7 +400,7 @@
 
         @pl.loop(0, 4)
         def _(j):
-            k = (j + 1) % 4
+            k = (j + 2) % 4
             there = (z + k) % 4
 
             @pl.loop(0, 2)
@@ -389,19 +412,22 @@
                 def _():
                     c_copy(e, k).start()
 
-            @pl.when(j > 0)
+            @pl.when(j == 1)
             def _():
-                over_z(e, j)
-
-        over_z(e, 0)
+                d_far_start(e)
+
+        d_cores(e, 3)
+        d_cores(e, 1)
+        d_near_start(e)
+        d_cores(e, 0)
 
     def o_copy(e):
         return remote(d_sum.at[e], d_out.at[e], o_send.at[e], o_recv.at[e], at(y_lo, z, y_hi, core, x))
 
     for e in range(2):
-        for k in (1, 3, 2):
-            d_copy(e, k).wait_recv()
-        d_sum[e] = d_part[e, core, z] + (d_got[e, 1] + d_got[e, 2] + d_got[e, 3])
+        d_copy(UP, e).wait_recv()
+        d_copy(DOWN, e).wait_recv()
+        d_sum[e] = d_part[e, core, z] + (d_got[0, e] + d_got[1, e])
 
         @pl.when(stays)
         def _():
@@ -434,10 +460,10 @@
 
         for k in (1, 2, 3):
             second(e, k).wait_send()
-            d_copy(e, k).wait_send()
         for kind in range(4):
             x_copy(kind, e).wait_send()
             c_copy(e, kind).wait_send()
+            d_copy(kind, e).wait_send()
             for side in range(2):
                 n_copy(kind, e, side).wait_send()
                 y_copy(kind, e, side).wait_send()
@@ -489,12 +515,13 @@
             pltpu.VMEM((2, 256, 896), BF),
             pltpu.VMEM((2, 2, 4, 256, 256), F32),
             pltpu.VMEM((2, 4, 256, 256), F32),
-            pltpu.VMEM((2, 4, 256, 256), F32),
+            pltpu.VMEM((2, 2, 128, 256), F32),
+            pltpu.VMEM((2, 2, 256, 256), F32),
             pltpu.VMEM((2, 256, 256), F32),
             pltpu.VMEM((2, 256, 256), F32),
             dma((2, 16)), dma((2, 16)), dma((2, 4)), dma((2, 4)), dma((2, 8)), dma((2, 8)), dma((6,)), dma((4, 2)), dma((4, 2)),
             dma((5, 4)), dma((5, 4)), dma((4, 2)), dma((4, 2)), dma((4, 2, 2)), dma((4, 2, 2)), dma((4, 2, 2)), dma((4, 2, 2)),
-            dma((2, 4)), dma((2, 4)), dma((2, 4)), dma((2, 4)), dma((2,)), dma((2,)),
+            dma((2, 4)), dma((2, 4)), dma((4, 2)), dma((4, 2)), dma((2,)), dma((2,)),
         ],
         compiler_params=pltpu.CompilerParams(collective_id=0, has_side_effects=True, vmem_limit_bytes=60 << 20),
         cost_estimate=pl.CostEstimate(

time: 162 us -> 158 us (0.975)
  Pallas kernels: 157 us -> 152 us
    pallas_call x1, Pallas kernels: 157 us -> 152 us  [on_device(): pl.pallas_call(kernel, out_shape=(jax.ShapeDtypeStruct((448, 512), F32),...]
where the time goes in v4:
time: 158 us; the launch traced here: 157 us
  Pallas kernels  152 us (96%)
  other arithmetic  4.41 us (3%)
    pallas_call x1, Pallas kernels, on_device(): pl.pallas_call(kernel, out_shape=(jax.ShapeDtypeStruct((448, 512), F32),...  152 us

profile of v4, /device:TPU:1, one launch (start us, length us, event | category | flops | bytes accessed | tf_op | source)
XLA Modules:
  0.0 157.4 jit_solution(11016011175047313862)
XLA Ops:
  0.6 1.3 select_reduce_fusion.inv_ref
  1.9 152.3 %selected_inverse.1 = (f32[448,512]{1,0:T(8,128)}, f32[2,2,128,256]{3,2,1,0:T(8,128)}) custom-call(s32[28]{0:T(128)} %select_reduce_fusion.inv_ref, f32[448,896]{1,0:T(8,128)} %k_ref.1, f32[7,8,8,512]{3,2,1,0:T(8,128)} %bitcast.3), custom_call_target="tpu_custom_call" | custom-call | flops 15502147584 | bytes 4194304 | tf_op jit(solution)/shard_map/selected_inverse/pallas_call | solution.py:492
  154.3 0.0 copy-start
  154.3 0.0 copy-start.1
  154.3 2.3 %neg.3 = f32[448,512]{1,0:T(8,128)} negate(f32[448,512]{1,0:T(8,128)} %get-tuple-element.4) | non-fusion elementwise | flops 229376 | bytes 1835008 | tf_op jit(solution)/shard_map/neg | solution.py:532
  156.6 0.0 copy-done
  156.6 0.0 copy-done.1
  156.6 0.9 bitcast_add_fusion
Async XLA Ops:
  154.3 2.3 %copy-start = (f32[512,256]{1,0:T(8,128)S(1)}, f32[512,256]{1,0:T(8,128)}, u32[]{:S(2)}) copy-start(f32[512,256]{1,0:T(8,128)} %param.6) | copy-start | bytes 1572868
  154.3 2.3 %copy-start.1 = (f32[2,2,128,256]{3,2,1,0:T(8,128)S(1)}, f32[2,2,128,256]{3,2,1,0:T(8,128)}, u32[]{:S(2)}) copy-start(f32[2,2,128,256]{3,2,1,0:T(8,128)} %get-tuple-element.5) | copy-start | bytes 1572868

commit v5 on v4

--- a/solution.py
+++ b/solution.py
@@ -318,29 +318,25 @@
         y_copy(HALF_DOWN, e, s).start()
 
     y_start(0, 0)
-    y_start(1, 0)
     k_pass(HALF_UP).wait_recv()
     k_pass(HALF_DOWN).wait_recv()
     take_k((y + 2) % 4, k_all.at[(y + 2) % 4])
 
     @pl.loop(0, 4)
-    def _(t):
-        r = (t % 2) * 2 + t // 2
+    def _(r):
         take_p(r, y_lo)
         n_put(r, theirs, n_dots(theirs * 2 + y_lo, y_lo), True)
 
-        @pl.when(t < 2)
-        def _():
-            n_far_start(t, theirs)
-
-        @pl.when(t >= 2)
-        def _():
-            n_near_start(t - 2, theirs)
-
+        @pl.when(r % 2 == 0)
+        def _():
+            n_far_start(r // 2, theirs)
+
+        @pl.when(r % 2 == 1)
+        def _():
+            n_near_start(r // 2, theirs)
+
+    y_start(1, 0)
     y_pass(0, 0)
-    y_start(0, 1)
-    y_pass(1, 0)
-    y_start(1, 1)
 
     for e in range(2):
         x_copy(HALF_UP, e).wait_recv()
@@ -353,6 +349,11 @@
             for e in range(2):
                 columns = slice(e * 128, (e + 1) * 128)
                 pz_high[there, rows, columns], pz_low[there, rows, columns] = split(p_z[e, there, half].reshape(448, 128))
+
+    y_start(0, 1)
+    y_pass(1, 0)
+    y_start(1, 1)
+    y_pass(0, 1)
 
     def c_copy(e, k):
         there = (z + k) % 4
@@ -387,7 +388,6 @@
 
     @pl.loop(0, 2)
     def _(e):
-        y_pass(e, 1)
         for kind in (HALF_UP, HALF_DOWN):
             for s in range(2):
                 y_copy(kind, e, s).wait_recv()
@@ -416,10 +416,19 @@
             def _():
                 d_far_start(e)
 
+            @pl.when(jnp.logical_and(j == 1, e == 0))
+            def _():
+                y_pass(1, 1)
+
+            @pl.when(jnp.logical_and(j == 0, e == 1))
+            def _():
+                d_near_start(0)
+
         d_cores(e, 3)
         d_cores(e, 1)
-        d_near_start(e)
         d_cores(e, 0)
+
+    d_near_start(1)
 
     def o_copy(e):
         return remote(d_sum.at[e], d_out.at[e], o_send.at[e], o_recv.at[e], at(y_lo, z, y_hi, core, x))

time: 158 us -> 161 us (1.019)
  Pallas kernels: 152 us -> 155 us
    pallas_call x1, Pallas kernels: 152 us -> 155 us  [on_device(): pl.pallas_call(kernel, out_shape=(jax.ShapeDtypeStruct((448, 512), F32),...]
where the time goes in v5:
time: 161 us; the launch traced here: 160 us
  Pallas kernels  155 us (96%)
  other arithmetic  4.41 us (3%)
    pallas_call x1, Pallas kernels, on_device(): pl.pallas_call(kernel, out_shape=(jax.ShapeDtypeStruct((448, 512), F32),...  155 us

profile of v5, /device:TPU:1, one launch (start us, length us, event | category | flops | bytes accessed | tf_op | source)
XLA Modules:
  0.0 160.3 jit_solution(2061043224352275941)
XLA Ops:
  0.6 1.3 select_reduce_fusion.inv_ref
  1.9 155.3 %selected_inverse.1 = (f32[448,512]{1,0:T(8,128)}, f32[2,2,128,256]{3,2,1,0:T(8,128)}) custom-call(s32[28]{0:T(128)} %select_reduce_fusion.inv_ref, f32[448,896]{1,0:T(8,128)} %k_ref.1, f32[7,8,8,512]{3,2,1,0:T(8,128)} %bitcast.3), custom_call_target="tpu_custom_call" | custom-call | flops 15502147584 | bytes 4194304 | tf_op jit(solution)/shard_map/selected_inverse/pallas_call | solution.py:501
  157.2 0.0 copy-start
  157.2 0.0 copy-start.1
  157.2 2.3 %neg.3 = f32[448,512]{1,0:T(8,128)} negate(f32[448,512]{1,0:T(8,128)} %get-tuple-element.4) | non-fusion elementwise | flops 229376 | bytes 1835008 | tf_op jit(solution)/shard_map/neg | solution.py:541
  159.5 0.0 copy-done
  159.5 0.0 copy-done.1
  159.5 0.9 bitcast_add_fusion
Async XLA Ops:
  157.2 2.3 %copy-start = (f32[512,256]{1,0:T(8,128)S(1)}, f32[512,256]{1,0:T(8,128)}, u32[]{:S(2)}) copy-start(f32[512,256]{1,0:T(8,128)} %param.6) | copy-start | bytes 1572868
  157.2 2.3 %copy-start.1 = (f32[2,2,128,256]{3,2,1,0:T(8,128)S(1)}, f32[2,2,128,256]{3,2,1,0:T(8,128)}, u32[]{:S(2)}) copy-start(f32[2,2,128,256]{3,2,1,0:T(8,128)} %get-tuple-element.5) | copy-start | bytes 1572868

commit v6 on v5

--- a/solution.py
+++ b/solution.py
@@ -27,10 +27,10 @@
 def kernel(
     inv_ref, k_ref, f_ref, n_ref, d_ref,
     k_all, k_high, k_low, sent_0, sent_1, picked, p_x, p_high, p_low, p_z, pz_high, pz_low,
-    n_part, n_far, n_got, n_all, t_high, t_low, d_part, d_core, d_far, d_got, d_sum, d_out,
+    n_part, n_far, n_got, n_all, t_high, t_low, d_part, d_core, d_far, d_got, d_sum,
     one_send, one_recv, two_send, two_recv, three_send, three_recv, local_sem, k_send, k_recv,
     z_send, z_recv, x_send, x_recv, n_send, n_recv, y_send, y_recv,
-    c_send, c_recv, d_send, d_recv, o_send, o_recv,
+    c_send, c_recv, d_send, d_recv, out_sem, o_send, o_recv,
 ):
     row, col = lax.axis_index("row"), lax.axis_index("col")
     x, y_lo = row % 4, row // 4
@@ -115,7 +115,10 @@
     def take_k(there, ref):
         k_high[there], k_low[there] = split(ref[...])
 
-    take_k(y, k_ref)
+    k_here = pltpu.make_async_copy(k_ref, k_all.at[y], local_sem.at[6])
+    k_here.start()
+    k_here.wait()
+    take_k(y, k_all.at[y])
 
     def second(e, k):
         to = (x + 4 - k) % 4
@@ -190,6 +193,15 @@
         copy(DOWN, r).wait_recv()
         copy(HALF_DOWN, r).start()
 
+    def z_start(e):
+        for p in range(2):
+            z_copy(UP, 2 * e + p).start()
+            z_copy(DOWN, 2 * e + p).start()
+
+    def x_start(e):
+        x_copy(UP, e).start()
+        x_copy(DOWN, e).start()
+
     def third_done(e):
         third_here(e).wait()
 
@@ -201,12 +213,11 @@
         second(e, 0).wait()
         for k in (1, 2, 3):
             second(e, k).wait_recv()
-        for p in range(2):
-            z_copy(UP, 2 * e + p).start()
-            z_copy(DOWN, 2 * e + p).start()
+        if e == 0:
+            z_start(0)
         third_done(e)
-        x_copy(UP, e).start()
-        x_copy(DOWN, e).start()
+        if e == 0:
+            x_start(0)
 
     def core_start(r):
         z_copy(HALF_UP, r).wait_recv()
@@ -215,20 +226,12 @@
 
     pass_on(z_copy, 0)
     pass_on(z_copy, 1)
+    z_start(1)
+    x_start(1)
+    pass_on(x_copy, 0)
     core_start(0)
-    pass_on(x_copy, 0)
     core_start(1)
-    for half in range(2):
-        k_copy(UP, half).wait_recv()
-    k_pass(HALF_UP).start()
-    for half in range(2):
-        k_copy(DOWN, half).wait_recv()
-    k_pass(HALF_DOWN).start()
     pass_on(z_copy, 2)
-    pass_on(z_copy, 3)
-    take_k((y + 3) % 4, k_all.at[(y + 3) % 4])
-    take_k((y + 1) % 4, k_all.at[(y + 1) % 4])
-    pass_on(x_copy, 1)
 
     def n_copy(kind, e, side):
         src, dst = {
@@ -252,43 +255,65 @@
         n_part[e, 2, side, 224:448] += n_far[1, e, side]
         n_copy(DOWN, e, side).start()
 
-    def take_p(r, half):
-        @pl.loop(0, 7)
-        def _(k):
-            rows = pl.ds(pl.multiple_of(k * 128, 128), 128)
-            for i in range(2):
-                columns = slice(i * 128, (i + 1) * 128)
-                p_high[half, rows, columns], p_low[half, rows, columns] = split(
-                    p_x[r // 2, r % 2, i, half, pl.ds(2 * k, 2)].reshape(128, 128)
-                )
-
-    def n_dots(there, half):
-        return three(k_high[there], k_low[there], p_high[half], p_low[half])
-
-    def n_put(r, side, value, add):
+    def take_p(r):
+        for half in range(2):
+
+            @pl.loop(0, 7)
+            def _(k):
+                rows = pl.ds(pl.multiple_of(k * 128, 128), 128)
+                for i in range(2):
+                    columns = slice(i * 128, (i + 1) * 128)
+                    p_high[r, half, rows, columns], p_low[r, half, rows, columns] = split(
+                        p_x[r // 2, r % 2, i, half, pl.ds(2 * k, 2)].reshape(128, 128)
+                    )
+
+    def n_dots(r, side, half, add):
+        there = side * 2 + half
+        value = three(k_high[there], k_low[there], p_high[r, half], p_low[r, half])
         for i in range(2):
             columns = value[:, i * 128 : (i + 1) * 128]
             n_part[r // 2, 2 * (r % 2) + i, side] = columns + n_part[r // 2, 2 * (r % 2) + i, side] if add else columns
 
+    def n_first(r):
+        z_copy(CORE, r).wait_recv()
+        take_p(r)
+        n_dots(r, y_hi, y_lo, False)
+
     theirs = 1 - y_hi
+
+    @pl.loop(0, 2)
+    def _(r):
+        n_first(r)
+
+    pass_on(z_copy, 3)
+    for half in range(2):
+        k_copy(UP, half).wait_recv()
+    k_pass(HALF_UP).start()
+    for half in range(2):
+        k_copy(DOWN, half).wait_recv()
+    k_pass(HALF_DOWN).start()
+    take_k((y + 3) % 4, k_all.at[(y + 3) % 4])
+    take_k((y + 1) % 4, k_all.at[(y + 1) % 4])
+    core_start(2)
+    pass_on(x_copy, 1)
 
     @pl.loop(0, 4)
     def _(r):
-        z_copy(CORE, r).wait_recv()
-
-        @pl.when(r < 2)
-        def _():
-            core_start(r + 2)
-
-        take_p(r, 0)
-        take_p(r, 1)
-        n_put(r, y_hi, n_dots(y, y_lo) + n_dots(y_hi * 2 + 1 - y_lo, 1 - y_lo), False)
+        @pl.when(r >= 2)
+        def _():
+            n_first(r)
+
+        n_dots(r, y_hi, 1 - y_lo, True)
 
         @pl.when(r % 2 == 0)
         def _():
             n_far_start(r // 2, y_hi)
 
-        n_put(r, theirs, n_dots(theirs * 2 + 1 - y_lo, 1 - y_lo), False)
+        @pl.when(r == 0)
+        def _():
+            core_start(3)
+
+        n_dots(r, theirs, 1 - y_lo, False)
 
         @pl.when(r % 2 == 1)
         def _():
@@ -323,37 +348,37 @@
     take_k((y + 2) % 4, k_all.at[(y + 2) % 4])
 
     @pl.loop(0, 4)
-    def _(r):
-        take_p(r, y_lo)
-        n_put(r, theirs, n_dots(theirs * 2 + y_lo, y_lo), True)
-
-        @pl.when(r % 2 == 0)
-        def _():
-            n_far_start(r // 2, theirs)
-
-        @pl.when(r % 2 == 1)
-        def _():
-            n_near_start(r // 2, theirs)
+    def _(t):
+        n_dots((t % 2) * 2 + t // 2, theirs, y_lo, True)
+
+        @pl.when(t < 2)
+        def _():
+            n_far_start(t, theirs)
+
+        @pl.when(t >= 2)
+        def _():
+            n_near_start(t - 2, theirs)
 
     y_start(1, 0)
     y_pass(0, 0)
 
-    for e in range(2):
+    def take_z(e):
         x_copy(HALF_UP, e).wait_recv()
         x_copy(HALF_DOWN, e).wait_recv()
 
-    @pl.loop(0, 4)
-    def _(there):
-        for half in range(2):
-            rows = slice(half * 448, (half + 1) * 448)
-            for e in range(2):
-                columns = slice(e * 128, (e + 1) * 128)
+        @pl.loop(0, 4)
+        def _(there):
+            for half in range(2):
+                rows, columns = slice(half * 448, (half + 1) * 448), slice(e * 128, (e + 1) * 128)
                 pz_high[there, rows, columns], pz_low[there, rows, columns] = split(p_z[e, there, half].reshape(448, 128))
 
+    take_z(0)
+    take_z(1)
     y_start(0, 1)
     y_pass(1, 0)
     y_start(1, 1)
     y_pass(0, 1)
+    y_pass(1, 1)
 
     def c_copy(e, k):
         there = (z + k) % 4
@@ -386,11 +411,18 @@
         d_part[e, core, (z + 3) % 4, 128:256] += d_far[1, e]
         d_copy(DOWN, e).start()
 
+    def n_out(e, half):
+        src = n_all.at[e, half * 2 + y_lo, pl.ds(pl.multiple_of(y_hi * 448, 64), 448)]
+        columns = pl.ds(pl.multiple_of(half * 256 + e * 128, 128), 128)
+        return pltpu.make_async_copy(src, n_ref.at[:, columns], out_sem.at[e, half])
+
     @pl.loop(0, 2)
     def _(e):
         for kind in (HALF_UP, HALF_DOWN):
             for s in range(2):
                 y_copy(kind, e, s).wait_recv()
+        for half in range(2):
+            n_out(e, half).start()
         for low in range(2):
             for high in range(2):
                 for k in range(7):
@@ -416,10 +448,6 @@
             def _():
                 d_far_start(e)
 
-            @pl.when(jnp.logical_and(j == 1, e == 0))
-            def _():
-                y_pass(1, 1)
-
             @pl.when(jnp.logical_and(j == 0, e == 1))
             def _():
                 d_near_start(0)
@@ -431,31 +459,23 @@
     d_near_start(1)
 
     def o_copy(e):
-        return remote(d_sum.at[e], d_out.at[e], o_send.at[e], o_recv.at[e], at(y_lo, z, y_hi, core, x))
+        return remote(d_sum.at[e], d_ref.at[:, e], o_send.at[e], o_recv.at[e], at(y_lo, z, y_hi, core, x))
+
+    def o_here(e):
+        return pltpu.make_async_copy(d_sum.at[e], d_ref.at[:, e], o_recv.at[e])
 
     for e in range(2):
         d_copy(UP, e).wait_recv()
         d_copy(DOWN, e).wait_recv()
-        d_sum[e] = d_part[e, core, z] + (d_got[0, e] + d_got[1, e])
+        d_sum[e] = (d_part[e, core, z] + (d_got[0, e] + d_got[1, e])).reshape(2, 128, 256)
 
         @pl.when(stays)
         def _():
-            pltpu.make_async_copy(d_sum.at[e], d_out.at[e], o_recv.at[e]).start()
+            o_here(e).start()
 
         @pl.when(jnp.logical_not(stays))
         def _():
             o_copy(e).start()
-
-    for e in range(2):
-        for half in range(2):
-            n_ref[:, half * 256 + e * 128 : half * 256 + (e + 1) * 128] = n_all[
-                e, half * 2 + y_lo, pl.ds(pl.multiple_of(y_hi * 448, 64), 448)
-            ]
-
-    for e in range(2):
-        pltpu.make_async_copy(d_sum.at[e], d_out.at[e], o_recv.at[e]).wait()
-        d_ref[0, e] = d_out[e, 0:128]
-        d_ref[1, e] = d_out[e, 128:256]
 
     for e in range(2):
 
@@ -492,17 +512,22 @@
         for kind in range(5):
             z_copy(kind, r).wait_send()
 
+    for e in range(2):
+        for half in range(2):
+            n_out(e, half).wait()
+        o_here(e).wait()
+
 
 def on_device(known_inverse, factor_panel, diag_base, ancestor_map):
     blocks = jnp.arange(28, dtype=jnp.int32)
     inverse = jnp.sum(jnp.where(ancestor_map[None, :] == blocks[:, None], blocks[None, :], 0), axis=1)
-    vmem = pl.BlockSpec(memory_space=pltpu.VMEM)
+    whole = pl.BlockSpec(memory_space=pl.ANY)
     dma = pltpu.SemaphoreType.DMA
     product, reduced = pl.pallas_call(
         kernel,
         out_shape=(jax.ShapeDtypeStruct((448, 512), F32), jax.ShapeDtypeStruct((2, 2, 128, 256), F32)),
-        in_specs=[pl.BlockSpec(memory_space=pltpu.SMEM), vmem, vmem],
-        out_specs=(vmem, vmem),
+        in_specs=[pl.BlockSpec(memory_space=pltpu.SMEM), whole, whole],
+        out_specs=(whole, whole),
         scratch_shapes=[
             pltpu.VMEM((4, 448, 896), F32),
             pltpu.VMEM((4, 448, 896), BF),
@@ -511,8 +536,8 @@
             pltpu.VMEM((112, 8, 128), F32),
             pltpu.VMEM((2, 2, 56, 8, 128), F32),
             pltpu.VMEM((2, 2, 2, 2, 14, 4, 2, 8, 128), F32),
-            pltpu.VMEM((2, 896, 256), BF),
-            pltpu.VMEM((2, 896, 256), BF),
+            pltpu.VMEM((4, 2, 896, 256), BF),
+            pltpu.VMEM((4, 2, 896, 256), BF),
             pltpu.VMEM((2, 4, 2, 7, 8, 8, 128), F32),
             pltpu.VMEM((4, 896, 256), BF),
             pltpu.VMEM((4, 896, 256), BF),
@@ -526,11 +551,10 @@
             pltpu.VMEM((2, 4, 256, 256), F32),
             pltpu.VMEM((2, 2, 128, 256), F32),
             pltpu.VMEM((2, 2, 256, 256), F32),
-            pltpu.VMEM((2, 256, 256), F32),
-            pltpu.VMEM((2, 256, 256), F32),
-            dma((2, 16)), dma((2, 16)), dma((2, 4)), dma((2, 4)), dma((2, 8)), dma((2, 8)), dma((6,)), dma((4, 2)), dma((4, 2)),
+            pltpu.VMEM((2, 2, 128, 256), F32),
+            dma((2, 16)), dma((2, 16)), dma((2, 4)), dma((2, 4)), dma((2, 8)), dma((2, 8)), dma((7,)), dma((4, 2)), dma((4, 2)),
             dma((5, 4)), dma((5, 4)), dma((4, 2)), dma((4, 2)), dma((4, 2, 2)), dma((4, 2, 2)), dma((4, 2, 2)), dma((4, 2, 2)),
-            dma((2, 4)), dma((2, 4)), dma((4, 2)), dma((4, 2)), dma((2,)), dma((2,)),
+            dma((2, 4)), dma((2, 4)), dma((4, 2)), dma((4, 2)), dma((2, 2)), dma((2,)), dma((2,)),
         ],
         compiler_params=pltpu.CompilerParams(collective_id=0, has_side_effects=True, vmem_limit_bytes=60 << 20),
         cost_estimate=pl.CostEstimate(

time: 161 us -> 153 us (0.950)
  Pallas kernels: 155 us -> 147 us
    pallas_call x1, Pallas kernels: 155 us -> 147 us  [on_device(): pl.pallas_call(kernel, out_shape=(jax.ShapeDtypeStruct((448, 512), F32),...]
where the time goes in v6:
time: 153 us; the launch traced here: 152 us
  Pallas kernels  147 us (96%)
  other arithmetic  4.41 us (3%)
    pallas_call x1, Pallas kernels, on_device(): pl.pallas_call(kernel, out_shape=(jax.ShapeDtypeStruct((448, 512), F32),...  147 us

profile of v6, /device:TPU:1, one launch (start us, length us, event | category | flops | bytes accessed | tf_op | source)
XLA Modules:
  0.0 152.5 jit_solution(13594108549102495438)
XLA Ops:
  0.6 1.3 select_reduce_fusion.inv_ref
  1.9 147.4 %selected_inverse.1 = (f32[448,512]{1,0:T(8,128)}, f32[2,2,128,256]{3,2,1,0:T(8,128)}) custom-call(s32[28]{0:T(128)} %select_reduce_fusion.inv_ref, f32[448,896]{1,0:T(8,128)} %k_ref.1, f32[7,8,8,512]{3,2,1,0:T(8,128)} %bitcast.3), custom_call_target="tpu_custom_call" | custom-call | flops 15502147584 | bytes 4194304 | tf_op jit(solution)/shard_map/selected_inverse/pallas_call | solution.py:526
  149.3 0.0 copy-start
  149.3 0.0 copy-start.1
  149.3 2.3 %neg.3 = f32[448,512]{1,0:T(8,128)} negate(f32[448,512]{1,0:T(8,128)} %get-tuple-element.4) | non-fusion elementwise | flops 229376 | bytes 1835008 | tf_op jit(solution)/shard_map/neg | solution.py:565
  151.6 0.0 copy-done
  151.6 0.0 copy-done.1
  151.6 0.9 bitcast_add_fusion
Async XLA Ops:
  149.3 2.3 %copy-start = (f32[512,256]{1,0:T(8,128)S(1)}, f32[512,256]{1,0:T(8,128)}, u32[]{:S(2)}) copy-start(f32[512,256]{1,0:T(8,128)} %param.6) | copy-start | bytes 1572868
  149.3 2.3 %copy-start.1 = (f32[2,2,128,256]{3,2,1,0:T(8,128)S(1)}, f32[2,2,128,256]{3,2,1,0:T(8,128)}, u32[]{:S(2)}) copy-start(f32[2,2,128,256]{3,2,1,0:T(8,128)} %get-tuple-element.5) | copy-start | bytes 1572868

commit v7 on v6

--- a/solution.py
+++ b/solution.py
@@ -10,6 +10,7 @@
 F32 = jnp.float32
 
 UP, DOWN, HALF_UP, HALF_DOWN, CORE = range(5)
+FREE_UP, FREE_DOWN = 4, 5
 
 
 def split(value):
@@ -139,6 +140,13 @@
         src = picked.at[e, :, pl.ds(place * 7, 7)]
         return pltpu.make_async_copy(src, p_z.at[e, x, :, :, place], local_sem.at[4 + e])
 
+    def third_start(e):
+        @pl.loop(1, 8)
+        def _(k):
+            third(e, k).start()
+
+        third_here(e).start()
+
     for e in range(2):
         first_here(e).wait()
 
@@ -150,13 +158,8 @@
             picked[e, j // 14, (j % 14) * 4 : (j % 14) * 4 + 4] = sent[e][pl.ds(inv_ref[j] * 4, 4)]
         for k in (1, 2, 3, 0):
             second(e, k).start()
-
-        @pl.loop(1, 8)
-        def _(k):
-            third(e, k).start()
-
-        third_here(e).start()
         if e == 0:
+            third_start(0)
             k_copy(UP, 1).start()
             k_copy(DOWN, 0).start()
 
@@ -209,43 +212,52 @@
         def _(k):
             third(e, k).wait_recv()
 
-    for e in range(2):
+    def second_done(e):
         second(e, 0).wait()
         for k in (1, 2, 3):
             second(e, k).wait_recv()
-        if e == 0:
-            z_start(0)
-        third_done(e)
-        if e == 0:
-            x_start(0)
+
+    second_done(0)
+    z_start(0)
+    third_start(1)
+    third_done(0)
+    x_start(0)
+    second_done(1)
+    pass_on(z_copy, 0)
+    pass_on(z_copy, 1)
+    z_start(1)
+    third_done(1)
+    x_start(1)
 
     def core_start(r):
         z_copy(HALF_UP, r).wait_recv()
         z_copy(HALF_DOWN, r).wait_recv()
         z_copy(CORE, r).start()
 
-    pass_on(z_copy, 0)
-    pass_on(z_copy, 1)
-    z_start(1)
-    x_start(1)
     pass_on(x_copy, 0)
     core_start(0)
     core_start(1)
-    pass_on(z_copy, 2)
 
     def n_copy(kind, e, side):
+        low, high = pl.ds(0, 224), pl.ds(224, 224)
         src, dst = {
-            HALF_UP: (n_part.at[e, 1, side, pl.ds(0, 224)], n_far.at[0, e, side]),
-            HALF_DOWN: (n_part.at[e, 1, side, pl.ds(224, 224)], n_far.at[1, e, side]),
-            UP: (n_part.at[e, 0, side], n_got.at[0, e, side]),
-            DOWN: (n_part.at[e, 2, side], n_got.at[1, e, side]),
+            HALF_UP: (n_part.at[e, 1, side, low], n_far.at[0, e, side]),
+            HALF_DOWN: (n_part.at[e, 1, side, high], n_far.at[1, e, side]),
+            UP: (n_part.at[e, 0, side, low], n_got.at[0, e, side, low]),
+            DOWN: (n_part.at[e, 2, side, high], n_got.at[1, e, side, high]),
+            FREE_UP: (n_part.at[e, 0, side, high], n_got.at[0, e, side, high]),
+            FREE_DOWN: (n_part.at[e, 2, side, low], n_got.at[1, e, side, low]),
         }[kind]
-        to = on_x(1 if kind in (UP, HALF_UP) else 3)
+        to = on_x(1 if kind in (UP, HALF_UP, FREE_UP) else 3)
         return remote(src, dst, n_send.at[kind, e, side], n_recv.at[kind, e, side], to)
 
     def n_far_start(e, side):
         n_copy(HALF_UP, e, side).start()
         n_copy(HALF_DOWN, e, side).start()
+
+    def n_free_start(e, side):
+        n_copy(FREE_UP, e, side).start()
+        n_copy(FREE_DOWN, e, side).start()
 
     def n_near_start(e, side):
         n_copy(HALF_UP, e, side).wait_recv()
@@ -270,54 +282,40 @@
     def n_dots(r, side, half, add):
         there = side * 2 + half
         value = three(k_high[there], k_low[there], p_high[r, half], p_low[r, half])
-        for i in range(2):
-            columns = value[:, i * 128 : (i + 1) * 128]
-            n_part[r // 2, 2 * (r % 2) + i, side] = columns + n_part[r // 2, 2 * (r % 2) + i, side] if add else columns
+
+        @pl.when(add)
+        def _():
+            for i in range(2):
+                n_part[r // 2, 2 * (r % 2) + i, side] += value[:, i * 128 : (i + 1) * 128]
+
+        @pl.when(jnp.logical_not(add))
+        def _():
+            for i in range(2):
+                n_part[r // 2, 2 * (r % 2) + i, side] = value[:, i * 128 : (i + 1) * 128]
 
     def n_first(r):
         z_copy(CORE, r).wait_recv()
         take_p(r)
-        n_dots(r, y_hi, y_lo, False)
 
     theirs = 1 - y_hi
 
     @pl.loop(0, 2)
     def _(r):
         n_first(r)
-
-    pass_on(z_copy, 3)
+        n_dots(r, y_hi, y_lo, r < 0)
+
+    pass_on(z_copy, 2)
     for half in range(2):
         k_copy(UP, half).wait_recv()
     k_pass(HALF_UP).start()
     for half in range(2):
         k_copy(DOWN, half).wait_recv()
     k_pass(HALF_DOWN).start()
+    pass_on(x_copy, 1)
+    pass_on(z_copy, 3)
     take_k((y + 3) % 4, k_all.at[(y + 3) % 4])
     take_k((y + 1) % 4, k_all.at[(y + 1) % 4])
     core_start(2)
-    pass_on(x_copy, 1)
-
-    @pl.loop(0, 4)
-    def _(r):
-        @pl.when(r >= 2)
-        def _():
-            n_first(r)
-
-        n_dots(r, y_hi, 1 - y_lo, True)
-
-        @pl.when(r % 2 == 0)
-        def _():
-            n_far_start(r // 2, y_hi)
-
-        @pl.when(r == 0)
-        def _():
-            core_start(3)
-
-        n_dots(r, theirs, 1 - y_lo, False)
-
-        @pl.when(r % 2 == 1)
-        def _():
-            n_near_start(r // 2, y_hi)
 
     def y_copy(kind, e, s):
         there = (y + {UP: 0, DOWN: 0, HALF_UP: 3, HALF_DOWN: 1}[kind]) % 4
@@ -329,8 +327,8 @@
 
     def y_start(e, s):
         side = (y_hi + s) % 2
-        n_copy(UP, e, side).wait_recv()
-        n_copy(DOWN, e, side).wait_recv()
+        for kind in (UP, DOWN, FREE_UP, FREE_DOWN):
+            n_copy(kind, e, side).wait_recv()
         rows = pl.ds(pl.multiple_of(side * 448, 64), 448)
         n_all[e, y, rows] = n_part[e, 3, side] + (n_got[0, e, side] + n_got[1, e, side])
         y_copy(UP, e, s).start()
@@ -342,24 +340,54 @@
         y_copy(DOWN, e, s).wait_recv()
         y_copy(HALF_DOWN, e, s).start()
 
-    y_start(0, 0)
+    @pl.loop(0, 10)
+    def _(q):
+        def after(step, action, *args):
+            @pl.when(q == step)
+            def _():
+                action(*args)
+
+        after(2, n_first, 2)
+        after(4, n_first, 3)
+        own_block = jnp.logical_or(q == 2, q == 4)
+        add = jnp.logical_or(q < 2, jnp.logical_or(q == 3, q == 5))
+        r = jnp.where(q < 2, q, jnp.where(q < 6, q // 2 + 1, q - 6))
+        n_dots(r, jnp.where(q < 6, y_hi, theirs), jnp.where(own_block, y_lo, 1 - y_lo), add)
+        after(0, n_far_start, 0, y_hi)
+        after(1, n_free_start, 0, y_hi)
+        after(1, core_start, 3)
+        after(3, n_far_start, 1, y_hi)
+        after(3, n_near_start, 0, y_hi)
+        after(5, n_free_start, 1, y_hi)
+        after(6, n_near_start, 1, y_hi)
+        after(8, y_start, 0, 0)
+
     k_pass(HALF_UP).wait_recv()
     k_pass(HALF_DOWN).wait_recv()
     take_k((y + 2) % 4, k_all.at[(y + 2) % 4])
 
     @pl.loop(0, 4)
     def _(t):
-        n_dots((t % 2) * 2 + t // 2, theirs, y_lo, True)
-
-        @pl.when(t < 2)
-        def _():
-            n_far_start(t, theirs)
-
-        @pl.when(t >= 2)
-        def _():
-            n_near_start(t - 2, theirs)
-
-    y_start(1, 0)
+        n_dots(t, theirs, y_lo, t >= 0)
+
+        @pl.when(t == 0)
+        def _():
+            n_far_start(0, theirs)
+
+        @pl.when(t == 1)
+        def _():
+            n_free_start(0, theirs)
+            y_start(1, 0)
+
+        @pl.when(t == 2)
+        def _():
+            n_near_start(0, theirs)
+            n_far_start(1, theirs)
+
+        @pl.when(t == 3)
+        def _():
+            n_free_start(1, theirs)
+
     y_pass(0, 0)
 
     def take_z(e):
@@ -375,6 +403,7 @@
     take_z(0)
     take_z(1)
     y_start(0, 1)
+    n_near_start(1, theirs)
     y_pass(1, 0)
     y_start(1, 1)
     y_pass(0, 1)
@@ -382,21 +411,25 @@
 
     def c_copy(e, k):
         there = (z + k) % 4
-        return remote(d_part.at[e, 1 - core, there], d_core.at[e, there], c_send.at[e, k], c_recv.at[e, k], other_core)
+        return remote(d_part.at[e, there, 1 - core], d_core.at[e, there], c_send.at[e, k], c_recv.at[e, k], other_core)
 
     def d_copy(kind, e):
+        low, high = pl.ds(0, 128), pl.ds(128, 128)
         src, dst = {
-            HALF_UP: (d_part.at[e, core, (z + 2) % 4, pl.ds(0, 128)], d_far.at[0, e]),
-            HALF_DOWN: (d_part.at[e, core, (z + 2) % 4, pl.ds(128, 128)], d_far.at[1, e]),
-            UP: (d_part.at[e, core, (z + 1) % 4], d_got.at[0, e]),
-            DOWN: (d_part.at[e, core, (z + 3) % 4], d_got.at[1, e]),
+            HALF_UP: (d_part.at[e, (z + 2) % 4, core, low], d_far.at[0, e]),
+            HALF_DOWN: (d_part.at[e, (z + 2) % 4, core, high], d_far.at[1, e]),
+            UP: (d_part.at[e, (z + 1) % 4, core, low], d_got.at[0, e, low]),
+            DOWN: (d_part.at[e, (z + 3) % 4, core, high], d_got.at[1, e, high]),
+            FREE_UP: (d_part.at[e, (z + 1) % 4, core, high], d_got.at[0, e, high]),
+            FREE_DOWN: (d_part.at[e, (z + 3) % 4, core, low], d_got.at[1, e, low]),
         }[kind]
-        return remote(src, dst, d_send.at[kind, e], d_recv.at[kind, e], on_z(1 if kind in (UP, HALF_UP) else 3))
+        to = on_z(1 if kind in (UP, HALF_UP, FREE_UP) else 3)
+        return remote(src, dst, d_send.at[kind, e], d_recv.at[kind, e], to)
 
     def d_cores(e, k):
         there = (z + k) % 4
         c_copy(e, k).wait_recv()
-        d_part[e, core, there] += d_core[e, there]
+        d_part[e, there, core] += d_core[e, there]
 
     def d_far_start(e):
         d_cores(e, 2)
@@ -405,10 +438,10 @@
 
     def d_near_start(e):
         d_copy(HALF_UP, e).wait_recv()
-        d_part[e, core, (z + 1) % 4, 0:128] += d_far[0, e]
+        d_part[e, (z + 1) % 4, core, 0:128] += d_far[0, e]
         d_copy(UP, e).start()
         d_copy(HALF_DOWN, e).wait_recv()
-        d_part[e, core, (z + 3) % 4, 128:256] += d_far[1, e]
+        d_part[e, (z + 3) % 4, core, 128:256] += d_far[1, e]
         d_copy(DOWN, e).start()
 
     def n_out(e, half):
@@ -427,33 +460,34 @@
             for high in range(2):
                 for k in range(7):
                     rows = slice(k * 128, (k + 1) * 128)
-                    lines = slice(high * 128, (high + 1) * 128)
-                    t_high[low, lines, rows], t_low[low, lines, rows] = split(n_all[e, 2 * high + low, rows].T)
+                    lines = slice((low * 2 + high) * 128, (low * 2 + high + 1) * 128)
+                    t_high[lines, rows], t_low[lines, rows] = split(n_all[e, 2 * high + low, rows].T)
 
         @pl.loop(0, 4)
         def _(j):
-            k = (j + 2) % 4
+            k = jnp.where(j == 0, 2, jnp.where(j == 1, 1, jnp.where(j == 2, 3, 0)))
             there = (z + k) % 4
-
-            @pl.loop(0, 2)
-            def _(turn):
-                low = (core + 1 + turn) % 2
-                d_part[e, low, there] = three(t_high[low], t_low[low], pz_high[there], pz_low[there])
-
-                @pl.when(turn == 0)
-                def _():
-                    c_copy(e, k).start()
+            d_part[e, there] = three(t_high[...], t_low[...], pz_high[there], pz_low[there]).reshape(2, 256, 256)
+            c_copy(e, k).start()
+
+            @pl.when(jnp.logical_and(j == 0, e == 1))
+            def _():
+                d_near_start(0)
 
             @pl.when(j == 1)
             def _():
                 d_far_start(e)
 
-            @pl.when(jnp.logical_and(j == 0, e == 1))
+            @pl.when(j == 2)
             def _():
-                d_near_start(0)
-
-        d_cores(e, 3)
-        d_cores(e, 1)
+                d_cores(e, 1)
+                d_copy(FREE_UP, e).start()
+
+            @pl.when(j == 3)
+            def _():
+                d_cores(e, 3)
+                d_copy(FREE_DOWN, e).start()
+
         d_cores(e, 0)
 
     d_near_start(1)
@@ -465,9 +499,9 @@
         return pltpu.make_async_copy(d_sum.at[e], d_ref.at[:, e], o_recv.at[e])
 
     for e in range(2):
-        d_copy(UP, e).wait_recv()
-        d_copy(DOWN, e).wait_recv()
-        d_sum[e] = (d_part[e, core, z] + (d_got[0, e] + d_got[1, e])).reshape(2, 128, 256)
+        for kind in (UP, DOWN, FREE_UP, FREE_DOWN):
+            d_copy(kind, e).wait_recv()
+        d_sum[e] = (d_part[e, z, core] + (d_got[0, e] + d_got[1, e])).reshape(2, 128, 256)
 
         @pl.when(stays)
         def _():
@@ -492,10 +526,12 @@
         for kind in range(4):
             x_copy(kind, e).wait_send()
             c_copy(e, kind).wait_send()
+            for side in range(2):
+                y_copy(kind, e, side).wait_send()
+        for kind in range(6):
             d_copy(kind, e).wait_send()
             for side in range(2):
                 n_copy(kind, e, side).wait_send()
-                y_copy(kind, e, side).wait_send()
 
         @pl.when(jnp.logical_not(stays))
         def _():
@@ -545,16 +581,16 @@
             pltpu.VMEM((2, 2, 2, 224, 128), F32),
             pltpu.VMEM((2, 2, 2, 448, 128), F32),
             pltpu.VMEM((2, 4, 896, 128), F32),
-            pltpu.VMEM((2, 256, 896), BF),
-            pltpu.VMEM((2, 256, 896), BF),
-            pltpu.VMEM((2, 2, 4, 256, 256), F32),
+            pltpu.VMEM((512, 896), BF),
+            pltpu.VMEM((512, 896), BF),
+            pltpu.VMEM((2, 4, 2, 256, 256), F32),
             pltpu.VMEM((2, 4, 256, 256), F32),
             pltpu.VMEM((2, 2, 128, 256), F32),
             pltpu.VMEM((2, 2, 256, 256), F32),
             pltpu.VMEM((2, 2, 128, 256), F32),
             dma((2, 16)), dma((2, 16)), dma((2, 4)), dma((2, 4)), dma((2, 8)), dma((2, 8)), dma((7,)), dma((4, 2)), dma((4, 2)),
-            dma((5, 4)), dma((5, 4)), dma((4, 2)), dma((4, 2)), dma((4, 2, 2)), dma((4, 2, 2)), dma((4, 2, 2)), dma((4, 2, 2)),
-            dma((2, 4)), dma((2, 4)), dma((4, 2)), dma((4, 2)), dma((2, 2)), dma((2,)), dma((2,)),
+            dma((5, 4)), dma((5, 4)), dma((4, 2)), dma((4, 2)), dma((6, 2, 2)), dma((6, 2, 2)), dma((4, 2, 2)), dma((4, 2, 2)),
+            dma((2, 4)), dma((2, 4)), dma((6, 2)), dma((6, 2)), dma((2, 2)), dma((2,)), dma((2,)),
         ],
         compiler_params=pltpu.CompilerParams(collective_id=0, has_side_effects=True, vmem_limit_bytes=60 << 20),
         cost_estimate=pl.CostEstimate(

time: 153 us -> 142 us (0.928)
  Pallas kernels: 147 us -> 137 us
    pallas_call x1, Pallas kernels: 147 us -> 137 us  [on_device(): pl.pallas_call(kernel, out_shape=(jax.ShapeDtypeStruct((448, 512), F32),...]
where the time goes in v7:
time: 142 us
  Pallas kernels  137 us (96%)
  other arithmetic  4.41 us (3%)
    pallas_call x1, Pallas kernels, on_device(): pl.pallas_call(kernel, out_shape=(jax.ShapeDtypeStruct((448, 512), F32),...  137 us

profile of v7, /device:TPU:1, one launch (start us, length us, event | category | flops | bytes accessed | tf_op | source)
XLA Modules:
  0.0 141.8 jit_solution(12757986291089997540)
XLA Ops:
  0.6 1.3 select_reduce_fusion.inv_ref
  1.9 136.7 %selected_inverse.1 = (f32[448,512]{1,0:T(8,128)}, f32[2,2,128,256]{3,2,1,0:T(8,128)}) custom-call(s32[28]{0:T(128)} %select_reduce_fusion.inv_ref, f32[448,896]{1,0:T(8,128)} %k_ref.1, f32[7,8,8,512]{3,2,1,0:T(8,128)} %bitcast.3), custom_call_target="tpu_custom_call" | custom-call | flops 15502147584 | bytes 4194304 | tf_op jit(solution)/shard_map/selected_inverse/pallas_call | solution.py:562
  138.6 0.0 copy-start
  138.6 0.0 copy-start.1
  138.6 2.3 %neg.3 = f32[448,512]{1,0:T(8,128)} negate(f32[448,512]{1,0:T(8,128)} %get-tuple-element.4) | non-fusion elementwise | flops 229376 | bytes 1835008 | tf_op jit(solution)/shard_map/neg | solution.py:601
  140.9 0.0 copy-done
  140.9 0.0 copy-done.1
  140.9 0.9 bitcast_add_fusion
Async XLA Ops:
  138.6 2.3 %copy-start = (f32[512,256]{1,0:T(8,128)S(1)}, f32[512,256]{1,0:T(8,128)}, u32[]{:S(2)}) copy-start(f32[512,256]{1,0:T(8,128)} %param.6) | copy-start | bytes 1572868
  138.6 2.3 %copy-start.1 = (f32[2,2,128,256]{3,2,1,0:T(8,128)S(1)}, f32[2,2,128,256]{3,2,1,0:T(8,128)}, u32[]{:S(2)}) copy-start(f32[2,2,128,256]{3,2,1,0:T(8,128)} %get-tuple-element.5) | copy-start | bytes 1572868

commit v8 on v7

--- a/solution.py
+++ b/solution.py
@@ -1,3 +1,5 @@
+import functools
+
 import jax
 import jax.numpy as jnp
 from jax import lax
@@ -347,20 +349,28 @@
             def _():
                 action(*args)
 
-        after(2, n_first, 2)
-        after(4, n_first, 3)
-        own_block = jnp.logical_or(q == 2, q == 4)
-        add = jnp.logical_or(q < 2, jnp.logical_or(q == 3, q == 5))
-        r = jnp.where(q < 2, q, jnp.where(q < 6, q // 2 + 1, q - 6))
-        n_dots(r, jnp.where(q < 6, y_hi, theirs), jnp.where(own_block, y_lo, 1 - y_lo), add)
+        def among(*steps):
+            return functools.reduce(jnp.logical_or, [q == step for step in steps])
+
+        after(3, n_first, 2)
+        after(6, n_first, 3)
+        partners = among(2, 5, 8, 9)
+        own_block = among(3, 6)
+        add = jnp.logical_not(jnp.logical_or(partners, own_block))
+        r = jnp.where(
+            partners,
+            jnp.where(q == 2, 0, jnp.where(q == 5, 1, q - 6)),
+            jnp.where(q < 2, q, jnp.where(q < 5, 2, 3)),
+        )
+        n_dots(r, jnp.where(partners, theirs, y_hi), jnp.where(own_block, y_lo, 1 - y_lo), add)
         after(0, n_far_start, 0, y_hi)
         after(1, n_free_start, 0, y_hi)
         after(1, core_start, 3)
-        after(3, n_far_start, 1, y_hi)
-        after(3, n_near_start, 0, y_hi)
-        after(5, n_free_start, 1, y_hi)
-        after(6, n_near_start, 1, y_hi)
-        after(8, y_start, 0, 0)
+        after(4, n_far_start, 1, y_hi)
+        after(4, n_near_start, 0, y_hi)
+        after(7, n_free_start, 1, y_hi)
+        after(8, n_near_start, 1, y_hi)
+        after(9, y_start, 0, 0)
 
     k_pass(HALF_UP).wait_recv()
     k_pass(HALF_DOWN).wait_recv()
@@ -377,12 +387,12 @@
         @pl.when(t == 1)
         def _():
             n_free_start(0, theirs)
+
+        @pl.when(t == 2)
+        def _():
+            n_far_start(1, theirs)
             y_start(1, 0)
-
-        @pl.when(t == 2)
-        def _():
             n_near_start(0, theirs)
-            n_far_start(1, theirs)
 
         @pl.when(t == 3)
         def _():
@@ -397,31 +407,30 @@
         @pl.loop(0, 4)
         def _(there):
             for half in range(2):
-                rows, columns = slice(half * 448, (half + 1) * 448), slice(e * 128, (e + 1) * 128)
-                pz_high[there, rows, columns], pz_low[there, rows, columns] = split(p_z[e, there, half].reshape(448, 128))
+                columns = slice(e * 128, (e + 1) * 128)
+                pz_high[there, half, :, columns], pz_low[there, half, :, columns] = split(
+                    p_z[e, there, half].reshape(448, 128)
+                )
 
     take_z(0)
     take_z(1)
-    y_start(0, 1)
     n_near_start(1, theirs)
     y_pass(1, 0)
-    y_start(1, 1)
-    y_pass(0, 1)
-    y_pass(1, 1)
+    y_start(0, 1)
 
     def c_copy(e, k):
         there = (z + k) % 4
         return remote(d_part.at[e, there, 1 - core], d_core.at[e, there], c_send.at[e, k], c_recv.at[e, k], other_core)
 
     def d_copy(kind, e):
-        low, high = pl.ds(0, 128), pl.ds(128, 128)
+        two, up_, down_ = ((z + k) % 4 for k in (2, 1, 3))
         src, dst = {
-            HALF_UP: (d_part.at[e, (z + 2) % 4, core, low], d_far.at[0, e]),
-            HALF_DOWN: (d_part.at[e, (z + 2) % 4, core, high], d_far.at[1, e]),
-            UP: (d_part.at[e, (z + 1) % 4, core, low], d_got.at[0, e, low]),
-            DOWN: (d_part.at[e, (z + 3) % 4, core, high], d_got.at[1, e, high]),
-            FREE_UP: (d_part.at[e, (z + 1) % 4, core, high], d_got.at[0, e, high]),
-            FREE_DOWN: (d_part.at[e, (z + 3) % 4, core, low], d_got.at[1, e, low]),
+            HALF_UP: (d_part.at[e, two, core, 0], d_far.at[0, e]),
+            HALF_DOWN: (d_part.at[e, two, core, 1], d_far.at[1, e]),
+            UP: (d_part.at[e, up_, core, 0], d_got.at[0, e, 0]),
+            DOWN: (d_part.at[e, down_, core, 1], d_got.at[1, e, 1]),
+            FREE_UP: (d_part.at[e, up_, core, 1], d_got.at[0, e, 1]),
+            FREE_DOWN: (d_part.at[e, down_, core, 0], d_got.at[1, e, 0]),
         }[kind]
         to = on_z(1 if kind in (UP, HALF_UP, FREE_UP) else 3)
         return remote(src, dst, d_send.at[kind, e], d_recv.at[kind, e], to)
@@ -438,10 +447,10 @@
 
     def d_near_start(e):
         d_copy(HALF_UP, e).wait_recv()
-        d_part[e, (z + 1) % 4, core, 0:128] += d_far[0, e]
+        d_part[e, (z + 1) % 4, core, 0] += d_far[0, e]
         d_copy(UP, e).start()
         d_copy(HALF_DOWN, e).wait_recv()
-        d_part[e, (z + 3) % 4, core, 128:256] += d_far[1, e]
+        d_part[e, (z + 3) % 4, core, 1] += d_far[1, e]
         d_copy(DOWN, e).start()
 
     def n_out(e, half):
@@ -449,34 +458,51 @@
         columns = pl.ds(pl.multiple_of(half * 256 + e * 128, 128), 128)
         return pltpu.make_async_copy(src, n_ref.at[:, columns], out_sem.at[e, half])
 
-    @pl.loop(0, 2)
-    def _(e):
+    def d_rows(e, s):
         for kind in (HALF_UP, HALF_DOWN):
-            for s in range(2):
-                y_copy(kind, e, s).wait_recv()
+            y_copy(kind, e, s).wait_recv()
+        for high in range(2):
+            for low in range(2):
+                lines = slice(low * 128, (low + 1) * 128)
+                for first_row, size in ((0, 128), (128, 128), (256, 128), (384, 64)):
+                    start = (high + s) % 2 * 448 + first_row
+                    value = n_all[e, 2 * high + low, start : start + size].T
+                    columns = slice(first_row, first_row + size)
+                    t_high[high, lines, columns], t_low[high, lines, columns] = split(value)
+
+    def d_dots(s, there, high):
+        side = (high + s) % 2
+        return three(t_high[high], t_low[high], pz_high[there, side], pz_low[there, side])
+
+    def d_early(e):
+        d_rows(e, 0)
+
+        @pl.loop(0, 8)
+        def _(q):
+            there, high = q // 2, q % 2
+            d_part[e, there, :, high] = d_dots(0, there, high).reshape(2, 128, 256)
+
+    def d_late(e):
+        d_rows(e, 1)
         for half in range(2):
             n_out(e, half).start()
-        for low in range(2):
-            for high in range(2):
-                for k in range(7):
-                    rows = slice(k * 128, (k + 1) * 128)
-                    lines = slice((low * 2 + high) * 128, (low * 2 + high + 1) * 128)
-                    t_high[lines, rows], t_low[lines, rows] = split(n_all[e, 2 * high + low, rows].T)
 
         @pl.loop(0, 4)
         def _(j):
             k = jnp.where(j == 0, 2, jnp.where(j == 1, 1, jnp.where(j == 2, 3, 0)))
             there = (z + k) % 4
-            d_part[e, there] = three(t_high[...], t_low[...], pz_high[there], pz_low[there]).reshape(2, 256, 256)
+
+            @pl.loop(0, 2)
+            def _(high):
+                d_part[e, there, :, high] += d_dots(1, there, high).reshape(2, 128, 256)
+
             c_copy(e, k).start()
-
-            @pl.when(jnp.logical_and(j == 0, e == 1))
-            def _():
-                d_near_start(0)
 
             @pl.when(j == 1)
             def _():
                 d_far_start(e)
+                if e == 0:
+                    y_pass(1, 1)
 
             @pl.when(j == 2)
             def _():
@@ -490,6 +516,13 @@
 
         d_cores(e, 0)
 
+    d_early(0)
+    y_pass(0, 1)
+    y_start(1, 1)
+    d_early(1)
+    d_late(0)
+    d_near_start(0)
+    d_late(1)
     d_near_start(1)
 
     def o_copy(e):
@@ -501,7 +534,7 @@
     for e in range(2):
         for kind in (UP, DOWN, FREE_UP, FREE_DOWN):
             d_copy(kind, e).wait_recv()
-        d_sum[e] = (d_part[e, z, core] + (d_got[0, e] + d_got[1, e])).reshape(2, 128, 256)
+        d_sum[e] = d_part[e, z, core] + (d_got[0, e] + d_got[1, e])
 
         @pl.when(stays)
         def _():
@@ -575,18 +608,18 @@
             pltpu.VMEM((4, 2, 896, 256), BF),
             pltpu.VMEM((4, 2, 896, 256), BF),
             pltpu.VMEM((2, 4, 2, 7, 8, 8, 128), F32),
-            pltpu.VMEM((4, 896, 256), BF),
-            pltpu.VMEM((4, 896, 256), BF),
+            pltpu.VMEM((4, 2, 448, 256), BF),
+            pltpu.VMEM((4, 2, 448, 256), BF),
             pltpu.VMEM((2, 4, 2, 448, 128), F32),
             pltpu.VMEM((2, 2, 2, 224, 128), F32),
             pltpu.VMEM((2, 2, 2, 448, 128), F32),
             pltpu.VMEM((2, 4, 896, 128), F32),
-            pltpu.VMEM((512, 896), BF),
-            pltpu.VMEM((512, 896), BF),
-            pltpu.VMEM((2, 4, 2, 256, 256), F32),
-            pltpu.VMEM((2, 4, 256, 256), F32),
+            pltpu.VMEM((2, 256, 448), BF),
+            pltpu.VMEM((2, 256, 448), BF),
+            pltpu.VMEM((2, 4, 2, 2, 128, 256), F32),
+            pltpu.VMEM((2, 4, 2, 128, 256), F32),
             pltpu.VMEM((2, 2, 128, 256), F32),
-            pltpu.VMEM((2, 2, 256, 256), F32),
+            pltpu.VMEM((2, 2, 2, 128, 256), F32),
             pltpu.VMEM((2, 2, 128, 256), F32),
             dma((2, 16)), dma((2, 16)), dma((2, 4)), dma((2, 4)), dma((2, 8)), dma((2, 8)), dma((7,)), dma((4, 2)), dma((4, 2)),
             dma((5, 4)), dma((5, 4)), dma((4, 2)), dma((4, 2)), dma((6, 2, 2)), dma((6, 2, 2)), dma((4, 2, 2)), dma((4, 2, 2)),

time: 142 us -> 140 us (0.986)
  Pallas kernels: 137 us -> 134 us
    pallas_call x1, Pallas kernels: 137 us -> 134 us  [on_device(): pl.pallas_call(kernel, out_shape=(jax.ShapeDtypeStruct((448, 512), F32),...]
where the time goes in v8:
time: 140 us; the launch traced here: 139 us
  Pallas kernels  134 us (96%)
  other arithmetic  4.41 us (3%)
    pallas_call x1, Pallas kernels, on_device(): pl.pallas_call(kernel, out_shape=(jax.ShapeDtypeStruct((448, 512), F32),...  134 us

profile of v8, /device:TPU:1, one launch (start us, length us, event | category | flops | bytes accessed | tf_op | source)
XLA Modules:
  0.0 139.3 jit_solution(7863102327428777845)
XLA Ops:
  0.6 1.3 select_reduce_fusion.inv_ref
  1.9 134.2 %selected_inverse.1 = (f32[448,512]{1,0:T(8,128)}, f32[2,2,128,256]{3,2,1,0:T(8,128)}) custom-call(s32[28]{0:T(128)} %select_reduce_fusion.inv_ref, f32[448,896]{1,0:T(8,128)} %k_ref.1, f32[7,8,8,512]{3,2,1,0:T(8,128)} %bitcast.3), custom_call_target="tpu_custom_call" | custom-call | flops 15502147584 | bytes 4194304 | tf_op jit(solution)/shard_map/selected_inverse/pallas_call | solution.py:595
  136.2 0.0 copy-start
  136.2 0.0 copy-start.1
  136.2 2.3 %neg.3 = f32[448,512]{1,0:T(8,128)} negate(f32[448,512]{1,0:T(8,128)} %get-tuple-element.4) | non-fusion elementwise | flops 229376 | bytes 1835008 | tf_op jit(solution)/shard_map/neg | solution.py:634
  138.5 0.0 copy-done
  138.5 0.0 copy-done.1
  138.5 0.9 bitcast_add_fusion
Async XLA Ops:
  136.2 2.3 %copy-start = (f32[512,256]{1,0:T(8,128)S(1)}, f32[512,256]{1,0:T(8,128)}, u32[]{:S(2)}) copy-start(f32[512,256]{1,0:T(8,128)} %param.6) | copy-start | bytes 1572868
  136.2 2.3 %copy-start.1 = (f32[2,2,128,256]{3,2,1,0:T(8,128)S(1)}, f32[2,2,128,256]{3,2,1,0:T(8,128)}, u32[]{:S(2)}) copy-start(f32[2,2,128,256]{3,2,1,0:T(8,128)} %get-tuple-element.5) | copy-start | bytes 1572868

commit v9 on v8

--- a/solution.py
+++ b/solution.py
@@ -28,7 +28,7 @@
 
 
 def kernel(
-    inv_ref, k_ref, f_ref, n_ref, d_ref,
+    map_ref, k_ref, f_ref, n_ref, d_ref,
     k_all, k_high, k_low, sent_0, sent_1, picked, p_x, p_high, p_low, p_z, pz_high, pz_low,
     n_part, n_far, n_got, n_all, t_high, t_low, d_part, d_core, d_far, d_got, d_sum,
     one_send, one_recv, two_send, two_recv, three_send, three_recv, local_sem, k_send, k_recv,
@@ -142,6 +142,9 @@
         src = picked.at[e, :, pl.ds(place * 7, 7)]
         return pltpu.make_async_copy(src, p_z.at[e, x, :, :, place], local_sem.at[4 + e])
 
+    stored = [map_ref[t] for t in range(28)]
+    inverse = [functools.reduce(jnp.maximum, [jnp.where(stored[t] == j, t, 0) for t in range(1, 28)]) for j in range(28)]
+
     def third_start(e):
         @pl.loop(1, 8)
         def _(k):
@@ -157,7 +160,7 @@
             first(e, k).wait_recv()
 
         for j in range(28):
-            picked[e, j // 14, (j % 14) * 4 : (j % 14) * 4 + 4] = sent[e][pl.ds(inv_ref[j] * 4, 4)]
+            picked[e, j // 14, (j % 14) * 4 : (j % 14) * 4 + 4] = sent[e][pl.ds(inverse[j] * 4, 4)]
         for k in (1, 2, 3, 0):
             second(e, k).start()
         if e == 0:
@@ -390,9 +393,9 @@
 
         @pl.when(t == 2)
         def _():
-            n_far_start(1, theirs)
             y_start(1, 0)
             n_near_start(0, theirs)
+            n_far_start(1, theirs)
 
         @pl.when(t == 3)
         def _():
@@ -414,9 +417,9 @@
 
     take_z(0)
     take_z(1)
+    y_start(0, 1)
     n_near_start(1, theirs)
     y_pass(1, 0)
-    y_start(0, 1)
 
     def c_copy(e, k):
         there = (z + k) % 4
@@ -498,22 +501,19 @@
 
             c_copy(e, k).start()
 
-            @pl.when(j == 1)
+            @pl.when(j == 2)
             def _():
                 d_far_start(e)
-                if e == 0:
-                    y_pass(1, 1)
-
-            @pl.when(j == 2)
+
+            @pl.when(j == 3)
             def _():
                 d_cores(e, 1)
                 d_copy(FREE_UP, e).start()
-
-            @pl.when(j == 3)
-            def _():
-                d_cores(e, 3)
-                d_copy(FREE_DOWN, e).start()
-
+                if e == 0:
+                    y_pass(1, 1)
+
+        d_cores(e, 3)
+        d_copy(FREE_DOWN, e).start()
         d_cores(e, 0)
 
     d_early(0)
@@ -523,7 +523,6 @@
     d_late(0)
     d_near_start(0)
     d_late(1)
-    d_near_start(1)
 
     def o_copy(e):
         return remote(d_sum.at[e], d_ref.at[:, e], o_send.at[e], o_recv.at[e], at(y_lo, z, y_hi, core, x))
@@ -531,7 +530,7 @@
     def o_here(e):
         return pltpu.make_async_copy(d_sum.at[e], d_ref.at[:, e], o_recv.at[e])
 
-    for e in range(2):
+    def o_start(e):
         for kind in (UP, DOWN, FREE_UP, FREE_DOWN):
             d_copy(kind, e).wait_recv()
         d_sum[e] = d_part[e, z, core] + (d_got[0, e] + d_got[1, e])
@@ -543,6 +542,10 @@
         @pl.when(jnp.logical_not(stays))
         def _():
             o_copy(e).start()
+
+    o_start(0)
+    d_near_start(1)
+    o_start(1)
 
     for e in range(2):
 
@@ -588,8 +591,6 @@
 
 
 def on_device(known_inverse, factor_panel, diag_base, ancestor_map):
-    blocks = jnp.arange(28, dtype=jnp.int32)
-    inverse = jnp.sum(jnp.where(ancestor_map[None, :] == blocks[:, None], blocks[None, :], 0), axis=1)
     whole = pl.BlockSpec(memory_space=pl.ANY)
     dma = pltpu.SemaphoreType.DMA
     product, reduced = pl.pallas_call(
@@ -630,7 +631,7 @@
             flops=6 * (448 * 1792 * 2048 + 256 * 1792 * 2048), bytes_accessed=4 << 20, transcendentals=0
         ),
         name="selected_inverse",
-    )(inverse, known_inverse, factor_panel.reshape(7, 8, 8, 512))
+    )(ancestor_map, known_inverse, factor_panel.reshape(7, 8, 8, 512))
     return (-product, diag_base + reduced.reshape(512, 256))
 
 

time: 140 us -> 137 us (0.979)
  no operation moved by 1% of the time
where the time goes in v9:
time: 137 us
  Pallas kernels  133 us (97%)
  other arithmetic  3.13 us (2%)
    pallas_call x1, Pallas kernels, on_device(): pl.pallas_call(kernel, out_shape=(jax.ShapeDtypeStruct((448, 512), F32),...  133 us

profile of v9, /device:TPU:1, one launch (start us, length us, event | category | flops | bytes accessed | tf_op | source)
XLA Modules:
  0.0 136.6 jit_solution(10219772461207488621)
XLA Ops:
  0.6 132.8 %selected_inverse.1 = (f32[448,512]{1,0:T(8,128)}, f32[2,2,128,256]{3,2,1,0:T(8,128)}) custom-call(s32[28]{0:T(128)} %map_ref.1, f32[448,896]{1,0:T(8,128)} %k_ref.1, f32[7,8,8,512]{3,2,1,0:T(8,128)} %bitcast.3), custom_call_target="tpu_custom_call" | custom-call | flops 15502147584 | bytes 4194304 | tf_op jit(solution)/shard_map/selected_inverse/pallas_call | solution.py:596
  133.5 0.0 copy-start
  133.5 0.0 copy-start.1
  133.5 2.3 %neg.3 = f32[448,512]{1,0:T(8,128)} negate(f32[448,512]{1,0:T(8,128)} %get-tuple-element.4) | non-fusion elementwise | flops 229376 | bytes 1835008 | tf_op jit(solution)/shard_map/neg | solution.py:635
  135.8 0.0 copy-done
  135.8 0.0 copy-done.1
  135.8 0.9 bitcast_add_fusion
Async XLA Ops:
  133.5 2.3 %copy-start = (f32[512,256]{1,0:T(8,128)S(1)}, f32[512,256]{1,0:T(8,128)}, u32[]{:S(2)}) copy-start(f32[512,256]{1,0:T(8,128)} %param.6) | copy-start | bytes 1572868
  133.5 2.3 %copy-start.1 = (f32[2,2,128,256]{3,2,1,0:T(8,128)S(1)}, f32[2,2,128,256]{3,2,1,0:T(8,128)}, u32[]{:S(2)}) copy-start(f32[2,2,128,256]{3,2,1,0:T(8,128)} %get-tuple-element.5) | copy-start | bytes 1572868

commit v10 on v9

--- a/solution.py
+++ b/solution.py
@@ -309,18 +309,16 @@
         n_first(r)
         n_dots(r, y_hi, y_lo, r < 0)
 
+    k_copy(UP, 0).wait_recv()
+    k_pass(HALF_UP).start()
+    k_copy(DOWN, 1).wait_recv()
+    k_pass(HALF_DOWN).start()
     pass_on(z_copy, 2)
-    for half in range(2):
-        k_copy(UP, half).wait_recv()
-    k_pass(HALF_UP).start()
-    for half in range(2):
-        k_copy(DOWN, half).wait_recv()
-    k_pass(HALF_DOWN).start()
     pass_on(x_copy, 1)
-    pass_on(z_copy, 3)
+    k_copy(UP, 1).wait_recv()
+    k_copy(DOWN, 0).wait_recv()
     take_k((y + 3) % 4, k_all.at[(y + 3) % 4])
     take_k((y + 1) % 4, k_all.at[(y + 1) % 4])
-    core_start(2)
 
     def y_copy(kind, e, s):
         there = (y + {UP: 0, DOWN: 0, HALF_UP: 3, HALF_DOWN: 1}[kind]) % 4
@@ -335,7 +333,7 @@
         for kind in (UP, DOWN, FREE_UP, FREE_DOWN):
             n_copy(kind, e, side).wait_recv()
         rows = pl.ds(pl.multiple_of(side * 448, 64), 448)
-        n_all[e, y, rows] = n_part[e, 3, side] + (n_got[0, e, side] + n_got[1, e, side])
+        n_all[e, y, rows] = -(n_part[e, 3, side] + (n_got[0, e, side] + n_got[1, e, side]))
         y_copy(UP, e, s).start()
         y_copy(DOWN, e, s).start()
 
@@ -368,12 +366,13 @@
         n_dots(r, jnp.where(partners, theirs, y_hi), jnp.where(own_block, y_lo, 1 - y_lo), add)
         after(0, n_far_start, 0, y_hi)
         after(1, n_free_start, 0, y_hi)
-        after(1, core_start, 3)
+        after(0, pass_on, z_copy, 3)
+        after(1, core_start, 2)
+        after(3, core_start, 3)
         after(4, n_far_start, 1, y_hi)
-        after(4, n_near_start, 0, y_hi)
+        after(5, n_near_start, 0, y_hi)
         after(7, n_free_start, 1, y_hi)
         after(8, n_near_start, 1, y_hi)
-        after(9, y_start, 0, 0)
 
     k_pass(HALF_UP).wait_recv()
     k_pass(HALF_DOWN).wait_recv()
@@ -386,6 +385,7 @@
         @pl.when(t == 0)
         def _():
             n_far_start(0, theirs)
+            y_start(0, 0)
 
         @pl.when(t == 1)
         def _():
@@ -593,7 +593,7 @@
 def on_device(known_inverse, factor_panel, diag_base, ancestor_map):
     whole = pl.BlockSpec(memory_space=pl.ANY)
     dma = pltpu.SemaphoreType.DMA
-    product, reduced = pl.pallas_call(
+    new_column, reduced = pl.pallas_call(
         kernel,
         out_shape=(jax.ShapeDtypeStruct((448, 512), F32), jax.ShapeDtypeStruct((2, 2, 128, 256), F32)),
         in_specs=[pl.BlockSpec(memory_space=pltpu.SMEM), whole, whole],
@@ -632,7 +632,7 @@
         ),
         name="selected_inverse",
     )(ancestor_map, known_inverse, factor_panel.reshape(7, 8, 8, 512))
-    return (-product, diag_base + reduced.reshape(512, 256))
+    return (new_column, diag_base - reduced.reshape(512, 256))
 
 
 def solution(mesh):

time: 137 us -> 137 us (level)
    neg x1 -> x0, other arithmetic: 2.27 us -> none  [on_device(): return (-product, diag_base + reduced.reshape(512, 256))]
    sub x0 -> x1, other arithmetic: none -> 1.98 us  [on_device(): return (new_column, diag_base - reduced.reshape(512, 256))]
where the time goes in v10:
time: 137 us; the launch traced here: 136 us
  Pallas kernels  133 us (97%)
  other arithmetic  1.98 us (1%)
    pallas_call x1, Pallas kernels, on_device(): pl.pallas_call(kernel, out_shape=(jax.ShapeDtypeStruct((448, 512), F32),...  133 us

profile of v10, /device:TPU:1, one launch (start us, length us, event | category | flops | bytes accessed | tf_op | source)
XLA Modules:
  0.0 136.4 jit_solution(396188201289492236)
XLA Ops:
  0.6 0.0 copy-start.1
  0.6 132.8 %selected_inverse.1 = (f32[448,512]{1,0:T(8,128)}, f32[2,2,128,256]{3,2,1,0:T(8,128)}) custom-call(s32[28]{0:T(128)} %map_ref.1, f32[448,896]{1,0:T(8,128)} %k_ref.1, f32[7,8,8,512]{3,2,1,0:T(8,128)} %bitcast.3), custom_call_target="tpu_custom_call" | custom-call | flops 15502147584 | bytes 4194304 | tf_op jit(solution)/shard_map/selected_inverse/pallas_call | solution.py:596
  133.5 0.0 copy-start
  133.5 0.0 copy-done.1
  133.5 2.0 %bitcast_subtract_fusion = f32[512,256]{1,0:T(8,128)} fusion(f32[512,256]{1,0:T(8,128)S(1)} %copy-done.1, f32[2,2,128,256]{3,2,1,0:T(8,128)} %get-tuple-element.5), kind=kLoop, calls=%fused_computation | loop fusion | flops 131072 | bytes 1572864 | tf_op jit(solution)/shard_map/sub | solution.py:635
  135.5 0.0 copy-done
  135.5 0.9 copy.7
Async XLA Ops:
  0.6 132.9 %copy-start.1 = (f32[512,256]{1,0:T(8,128)S(1)}, f32[512,256]{1,0:T(8,128)}, u32[]{:S(2)}) copy-start(f32[512,256]{1,0:T(8,128)} %param.6) | copy-start | bytes 1572868
  133.5 2.0 %copy-start = (f32[448,512]{1,0:T(8,128)S(1)}, f32[448,512]{1,0:T(8,128)}, u32[]{:S(2)}) copy-start(f32[448,512]{1,0:T(8,128)} %get-tuple-element.8) | copy-start | bytes 2752516

commit v11 on v10

--- a/solution.py
+++ b/solution.py
@@ -163,8 +163,8 @@
             picked[e, j // 14, (j % 14) * 4 : (j % 14) * 4 + 4] = sent[e][pl.ds(inverse[j] * 4, 4)]
         for k in (1, 2, 3, 0):
             second(e, k).start()
+        third_start(e)
         if e == 0:
-            third_start(0)
             k_copy(UP, 1).start()
             k_copy(DOWN, 0).start()
 
@@ -224,24 +224,24 @@
 
     second_done(0)
     z_start(0)
-    third_start(1)
     third_done(0)
     x_start(0)
     second_done(1)
+    third_done(1)
+    x_start(1)
     pass_on(z_copy, 0)
+    pass_on(x_copy, 0)
     pass_on(z_copy, 1)
     z_start(1)
-    third_done(1)
-    x_start(1)
 
     def core_start(r):
         z_copy(HALF_UP, r).wait_recv()
         z_copy(HALF_DOWN, r).wait_recv()
         z_copy(CORE, r).start()
 
-    pass_on(x_copy, 0)
     core_start(0)
     core_start(1)
+    pass_on(x_copy, 1)
 
     def n_copy(kind, e, side):
         low, high = pl.ds(0, 224), pl.ds(224, 224)
@@ -314,7 +314,6 @@
     k_copy(DOWN, 1).wait_recv()
     k_pass(HALF_DOWN).start()
     pass_on(z_copy, 2)
-    pass_on(x_copy, 1)
     k_copy(UP, 1).wait_recv()
     k_copy(DOWN, 0).wait_recv()
     take_k((y + 3) % 4, k_all.at[(y + 3) % 4])
@@ -543,8 +542,8 @@
         def _():
             o_copy(e).start()
 
+    d_near_start(1)
     o_start(0)
-    d_near_start(1)
     o_start(1)
 
     for e in range(2):

time: 137 us -> 136 us (level)
  no operation moved by 1% of the time
where the time goes in v11:
time: 136 us
  Pallas kernels  132 us (97%)
  other arithmetic  1.98 us (1%)
    pallas_call x1, Pallas kernels, on_device(): pl.pallas_call(kernel, out_shape=(jax.ShapeDtypeStruct((448, 512), F32),...  132 us

profile of v11, /device:TPU:1, one launch (start us, length us, event | category | flops | bytes accessed | tf_op | source)
XLA Modules:
  0.0 135.8 jit_solution(9054897301693716917)
XLA Ops:
  0.6 0.0 copy-start.1
  0.6 132.2 %selected_inverse.1 = (f32[448,512]{1,0:T(8,128)}, f32[2,2,128,256]{3,2,1,0:T(8,128)}) custom-call(s32[28]{0:T(128)} %map_ref.1, f32[448,896]{1,0:T(8,128)} %k_ref.1, f32[7,8,8,512]{3,2,1,0:T(8,128)} %bitcast.3), custom_call_target="tpu_custom_call" | custom-call | flops 15502147584 | bytes 4194304 | tf_op jit(solution)/shard_map/selected_inverse/pallas_call | solution.py:595
  132.8 0.0 copy-start
  132.8 0.0 copy-done.1
  132.8 2.0 %bitcast_subtract_fusion = f32[512,256]{1,0:T(8,128)} fusion(f32[512,256]{1,0:T(8,128)S(1)} %copy-done.1, f32[2,2,128,256]{3,2,1,0:T(8,128)} %get-tuple-element.5), kind=kLoop, calls=%fused_computation | loop fusion | flops 131072 | bytes 1572864 | tf_op jit(solution)/shard_map/sub | solution.py:634
  134.8 0.0 copy-done
  134.8 0.9 copy.7
Async XLA Ops:
  0.6 132.2 %copy-start.1 = (f32[512,256]{1,0:T(8,128)S(1)}, f32[512,256]{1,0:T(8,128)}, u32[]{:S(2)}) copy-start(f32[512,256]{1,0:T(8,128)} %param.6) | copy-start | bytes 1572868
  132.8 2.0 %copy-start = (f32[448,512]{1,0:T(8,128)S(1)}, f32[448,512]{1,0:T(8,128)}, u32[]{:S(2)}) copy-start(f32[448,512]{1,0:T(8,128)} %get-tuple-element.8) | copy-start | bytes 2752516

commit v12 on v11

--- a/solution.py
+++ b/solution.py
@@ -93,14 +93,6 @@
     def first_here(e):
         return pltpu.make_async_copy(piece(col, e), sent[e].at[pl.ds(col * 7, 7)], local_sem.at[e])
 
-    for e in range(2):
-
-        @pl.loop(1, 16)
-        def _(k):
-            first(e, k).start()
-
-        first_here(e).start()
-
     def k_copy(kind, half):
         rows = pl.ds(half * 224, 224)
         return remote(
@@ -114,6 +106,14 @@
 
     k_copy(UP, 0).start()
     k_copy(DOWN, 1).start()
+
+    for e in range(2):
+
+        @pl.loop(1, 16)
+        def _(k):
+            first(e, k).start()
+
+        first_here(e).start()
 
     def take_k(there, ref):
         k_high[there], k_low[there] = split(ref[...])
@@ -500,7 +500,7 @@
 
             c_copy(e, k).start()
 
-            @pl.when(j == 2)
+            @pl.when(j == (2 if e == 0 else 1))
             def _():
                 d_far_start(e)
 

time: 136 us -> 153 us (1.12)
  Pallas kernels: 132 us -> 149 us
    pallas_call x1, Pallas kernels: 132 us -> 149 us  [on_device(): pl.pallas_call(kernel, out_shape=(jax.ShapeDtypeStruct((448, 512), F32),...]
where the time goes in v12:
time: 153 us
  Pallas kernels  149 us (97%)
  other arithmetic  1.98 us (1%)
    pallas_call x1, Pallas kernels, on_device(): pl.pallas_call(kernel, out_shape=(jax.ShapeDtypeStruct((448, 512), F32),...  149 us

profile of v12, /device:TPU:1, one launch (start us, length us, event | category | flops | bytes accessed | tf_op | source)
XLA Modules:
  0.0 152.8 jit_solution(7253315684751665582)
XLA Ops:
  0.6 0.0 copy-start.1
  0.6 149.2 %selected_inverse.1 = (f32[448,512]{1,0:T(8,128)}, f32[2,2,128,256]{3,2,1,0:T(8,128)}) custom-call(s32[28]{0:T(128)} %map_ref.1, f32[448,896]{1,0:T(8,128)} %k_ref.1, f32[7,8,8,512]{3,2,1,0:T(8,128)} %bitcast.3), custom_call_target="tpu_custom_call" | custom-call | flops 15502147584 | bytes 4194304 | tf_op jit(solution)/shard_map/selected_inverse/pallas_call | solution.py:595
  149.9 0.0 copy-start
  149.9 0.0 copy-done.1
  149.9 2.0 %bitcast_subtract_fusion = f32[512,256]{1,0:T(8,128)} fusion(f32[512,256]{1,0:T(8,128)S(1)} %copy-done.1, f32[2,2,128,256]{3,2,1,0:T(8,128)} %get-tuple-element.5), kind=kLoop, calls=%fused_computation | loop fusion | flops 131072 | bytes 1572864 | tf_op jit(solution)/shard_map/sub | solution.py:634
  151.9 0.0 copy-done
  151.9 0.9 copy.7
Async XLA Ops:
  0.6 149.2 %copy-start.1 = (f32[512,256]{1,0:T(8,128)S(1)}, f32[512,256]{1,0:T(8,128)}, u32[]{:S(2)}) copy-start(f32[512,256]{1,0:T(8,128)} %param.6) | copy-start | bytes 1572868
  149.9 2.0 %copy-start = (f32[448,512]{1,0:T(8,128)S(1)}, f32[448,512]{1,0:T(8,128)}, u32[]{:S(2)}) copy-start(f32[448,512]{1,0:T(8,128)} %get-tuple-element.8) | copy-start | bytes 2752516
